TPU v7x, 512 devices: a whole 4x4x16 slice. The times are simulated.
512 devices in a mesh: ctx: 128 (over z, x, y_hi), head: 4 (over y_lo, core).
Axes of the slice: x: 4, y: 4 (y_hi: 2, y_lo: 2; y = y_hi * 2 + y_lo), z: 16, core: 2. Of those that a mesh axis runs over, the one named last changes fastest.
Arguments:
- win_q: bfloat16 [16384, 4096], P('ctx', 'head'), may hold values from -5.5 to 5.5, as said below
- win_k: bfloat16 [16384, 512], P(('ctx', 'head')), may hold values from -5.5 to 5.5, as said below
- win_v: bfloat16 [16384, 512], P(('ctx', 'head')), may hold values from -6 to 6
- win_dout: bfloat16 [16384, 4096], P('ctx', 'head'), may hold values from -32 to 32
- full_q: bfloat16 [16384, 4096], P('ctx', 'head'), may hold values from -5.5 to 5.5, as said below
- full_k: bfloat16 [16384, 512], P(('ctx', 'head')), may hold values from -5.5 to 5.5, as said below
- full_v: bfloat16 [16384, 512], P(('ctx', 'head')), may hold values from -6 to 6
- full_dout: bfloat16 [16384, 4096], P('ctx', 'head'), may hold values from -32 to 32
- sinks: float32 [2, 64], P(None, 'head'), may hold values from 0 to 3
- segments: int32 [16384], replicated, may hold values from 0 to 31, never falling along the last dimension, each value on 1 to 768 neighbouring positions
Outputs:
- win_dq: bfloat16 [16384, 4096], P('ctx', 'head')
- win_dk: bfloat16 [16384, 512], P(('ctx', 'head'))
- win_dv: bfloat16 [16384, 512], P(('ctx', 'head'))
- full_dq: bfloat16 [16384, 4096], P('ctx', 'head')
- full_dk: bfloat16 [16384, 512], P(('ctx', 'head'))
- full_dv: bfloat16 [16384, 512], P(('ctx', 'head'))
- sink_grads: float32 [2, 64], P(None, 'head')
Inputs may be any that keep to these rules, and one draw needn't show every extreme that they name: `segments`: document numbers never fall along the sequence, every number is used, each document has 1 to 768 tokens and one has exactly 768. `win_q`: query features. `win_k`: key features. `full_q`: query features. `full_k`: key features.
All inputs are finite; a program needn't handle non-finite values.
Results may differ from a plain program's by a relative error of at most 0.012.
The roundings to bfloat16 on the way count: a program that leaves them out, or rounds other values in their place, can miss the bound.
Values may be sent and summed in bfloat16 or wider, within the bound.
No kernel may reach another device: no remote copies, remote signals or barrier semaphores. Data moves between devices by JAX's collectives and lax.ppermute only.
A program may use at most 64 MiB of HBM per device.

v0:
```python
import jax
import jax.numpy as jnp
from jax import lax
from jax.sharding import PartitionSpec as P

HEAD_DIM = 64
WINDOW = 128
CYCLE = 4
GROUP = 8


NEG = -1e30


def passed_along(shard, axis, by):
    size = lax.axis_size(axis)
    pairs = [(i, i + by) for i in range(size) if 0 <= i + by < size]
    return lax.ppermute(shard, axis, pairs)


def masked_scores(queries, key_rows, allowed, scaling):
    raw = jnp.einsum("qgd,kd->gqk", queries, key_rows, preferred_element_type=jnp.float32)
    return jnp.where(allowed[None], scaling * raw, NEG)


def softmax_rows(scores, sink_logit):
    row_max = jnp.maximum(jnp.max(scores, axis=-1), sink_logit[:, None])
    exponent = jnp.exp(scores - row_max[..., None])
    sink_term = jnp.exp(sink_logit[:, None] - row_max)
    row_total = jnp.sum(exponent, axis=-1) + sink_term
    return (exponent / row_total[..., None], sink_term / row_total)


def row_deltas(cotangent, output):
    return jnp.sum(cotangent.astype(jnp.float32) * output, axis=-1).T


def weighted_values(softmax, value_rows):
    return jnp.einsum(
        "gqk,kd->qgd", softmax.astype(jnp.bfloat16), value_rows, preferred_element_type=jnp.float32
    )


def block_grads(softmax, row_delta, queries, cotangent, key_rows, value_rows, scaling):
    weights = softmax.astype(jnp.bfloat16)
    weight_grads = jnp.einsum(
        "qgd,kd->gqk", cotangent, value_rows, preferred_element_type=jnp.float32
    )
    score_grads = (softmax * (weight_grads - row_delta[..., None])).astype(jnp.bfloat16)
    query_grads = scaling * jnp.einsum(
        "gqk,kd->qgd", score_grads, key_rows, preferred_element_type=jnp.float32
    )
    key_grads = scaling * jnp.einsum(
        "gqk,qgd->kd", score_grads, queries, preferred_element_type=jnp.float32
    )
    value_grads = jnp.einsum("gqk,qgd->kd", weights, cotangent, preferred_element_type=jnp.float32)
    return (query_grads, key_grads, value_grads)


def head_dense(queries, cotangent, key_rows, value_rows, allowed, sink_logit, scaling):
    softmax, sink_share = softmax_rows(
        masked_scores(queries, key_rows, allowed, scaling), sink_logit
    )
    output = weighted_values(softmax, value_rows)
    row_delta = row_deltas(cotangent, output)
    query_grads, key_grads, value_grads = block_grads(
        softmax, row_delta, queries, cotangent, key_rows, value_rows, scaling
    )
    return (query_grads, key_grads, value_grads, -jnp.sum(sink_share * row_delta, axis=-1))


def layer_grads(queries, cotangent, key_list, value_list, allowed_list, sink_logit, scaling):
    head_queries = jnp.moveaxis(queries, 1, 0)
    head_cotangent = jnp.moveaxis(cotangent, 1, 0)
    head_keys = tuple((jnp.moveaxis(key_rows, 1, 0) for key_rows in key_list))
    head_values = tuple((jnp.moveaxis(value_rows, 1, 0) for value_rows in value_list))
    allowed_all = jnp.concatenate(allowed_list, axis=1)

    def one_head(operands):
        return head_dense(
            operands[0], operands[1], operands[2], operands[3], allowed_all, operands[4], scaling
        )

    query_grads, key_grads, value_grads, sink_grads = lax.map(
        one_head,
        (
            head_queries,
            head_cotangent,
            jnp.concatenate(head_keys, axis=1),
            jnp.concatenate(head_values, axis=1),
            sink_logit,
        ),
    )
    cut_points = []
    running = 0
    for key_rows in key_list[:-1]:
        running = running + key_rows.shape[0]
        cut_points.append(running)
    key_parts = jnp.split(key_grads, cut_points, axis=1)
    value_parts = jnp.split(value_grads, cut_points, axis=1)
    row_count = queries.shape[0]
    query_out = jnp.moveaxis(query_grads, 0, 1).reshape(row_count, -1)
    key_out = [jnp.moveaxis(piece, 0, 1).reshape(piece.shape[1], -1) for piece in key_parts]
    value_out = [jnp.moveaxis(piece, 0, 1).reshape(piece.shape[1], -1) for piece in value_parts]
    return (query_out, key_out, value_out, sink_grads.reshape(-1))


def body(win_q, win_k, win_v, win_dout, full_q, full_k, full_v, full_dout, sinks, segments):
    scaling = HEAD_DIM ** (-0.5)
    local_kv = (
        lax.all_to_all(win_k, "head", split_axis=1, concat_axis=0, tiled=True),
        lax.all_to_all(win_v, "head", split_axis=1, concat_axis=0, tiled=True),
        lax.all_to_all(full_k, "head", split_axis=1, concat_axis=0, tiled=True),
        lax.all_to_all(full_v, "head", split_axis=1, concat_axis=0, tiled=True),
    )
    win_keys, win_values, full_keys, full_values = local_kv
    row_count = full_q.shape[0]
    kv_local = full_keys.shape[1] // HEAD_DIM
    cycle_index = lax.axis_index("ctx")
    row_start = cycle_index * row_count
    query_pos = row_start + jnp.arange(row_count, dtype=jnp.int32)
    query_seg = lax.dynamic_slice_in_dim(segments, row_start, row_count)
    halo_keys, halo_values = passed_along((win_keys, win_values), "ctx", 1)
    first_keys, first_values = passed_along((full_keys, full_values), "ctx", 1)
    fetched = [(first_keys, first_values)]
    for distance in range(2, CYCLE + 1):
        fetched.append(passed_along((full_keys, full_values), "ctx", distance))
    ordered = [fetched[CYCLE - 1 - offset] for offset in range(CYCLE)] + [(full_keys, full_values)]
    full_pad = jnp.concatenate([jnp.full((CYCLE * row_count,), -1, jnp.int32), segments])
    full_allowed = []
    for offset in range(CYCLE + 1):
        key_pos = row_start + (offset - CYCLE) * row_count + jnp.arange(row_count, dtype=jnp.int32)
        key_seg = lax.dynamic_slice_in_dim(full_pad, row_start + offset * row_count, row_count)
        full_allowed.append(
            (key_pos[None, :] <= query_pos[:, None]) & (key_seg[None, :] == query_seg[:, None])
        )
    head_shape = (row_count, kv_local, GROUP, HEAD_DIM)
    full_dq, full_kparts, full_vparts, full_dsink = layer_grads(
        full_q.reshape(head_shape),
        full_dout.reshape(head_shape),
        [pair[0].reshape(-1, kv_local, HEAD_DIM) for pair in ordered],
        [pair[1].reshape(-1, kv_local, HEAD_DIM) for pair in ordered],
        full_allowed,
        sinks[1].reshape(kv_local, GROUP),
        scaling,
    )
    win_pad = jnp.concatenate([jnp.full((WINDOW,), -1, jnp.int32), segments])
    halo_pos = row_start - WINDOW + jnp.arange(WINDOW, dtype=jnp.int32)
    halo_seg = lax.dynamic_slice_in_dim(win_pad, row_start, WINDOW)
    window_floor = query_pos[:, None] - WINDOW
    halo_allowed = (halo_pos[None, :] > window_floor) & (halo_seg[None, :] == query_seg[:, None])
    own_allowed = (
        (query_pos[None, :] <= query_pos[:, None])
        & (query_pos[None, :] > window_floor)
        & (query_seg[None, :] == query_seg[:, None])
    )
    win_dq, win_kparts, win_vparts, win_dsink = layer_grads(
        win_q.reshape(head_shape),
        win_dout.reshape(head_shape),
        [halo_keys.reshape(-1, kv_local, HEAD_DIM), win_keys.reshape(-1, kv_local, HEAD_DIM)],
        [halo_values.reshape(-1, kv_local, HEAD_DIM), win_values.reshape(-1, kv_local, HEAD_DIM)],
        [halo_allowed, own_allowed],
        sinks[0].reshape(kv_local, GROUP),
        scaling,
    )
    extra_keys = jnp.zeros_like(full_kparts[CYCLE])
    extra_values = jnp.zeros_like(full_vparts[CYCLE])
    lead_keys, lead_values = (full_kparts[CYCLE - 1], full_vparts[CYCLE - 1])
    for distance in range(2, CYCLE + 1):
        moved = (
            passed_along(
                full_kparts[CYCLE - distance].astype(jnp.bfloat16), "ctx", -distance
            ).astype(jnp.float32),
            passed_along(
                full_vparts[CYCLE - distance].astype(jnp.bfloat16), "ctx", -distance
            ).astype(jnp.float32),
        )
        extra_keys = extra_keys + moved[0]
        extra_values = extra_values + moved[1]
    returned = (
        passed_along(lead_keys.astype(jnp.bfloat16), "ctx", -1).astype(lead_keys.dtype),
        passed_along(lead_values.astype(jnp.bfloat16), "ctx", -1).astype(lead_values.dtype),
    ) + (
        passed_along(win_kparts[0].astype(jnp.bfloat16), "ctx", -1).astype(jnp.float32),
        passed_along(win_vparts[0].astype(jnp.bfloat16), "ctx", -1).astype(jnp.float32),
    )
    full_dk = full_kparts[CYCLE] + returned[0] + extra_keys
    full_dv = full_vparts[CYCLE] + returned[1] + extra_values
    win_dk = win_kparts[1] + returned[2]
    win_dv = win_vparts[1] + returned[3]
    sink_total = lax.psum(jnp.stack([win_dsink, full_dsink]), "ctx")
    grads_back = (
        lax.all_to_all(
            win_dk.astype(jnp.bfloat16), "head", split_axis=0, concat_axis=1, tiled=True
        ),
        lax.all_to_all(
            win_dv.astype(jnp.bfloat16), "head", split_axis=0, concat_axis=1, tiled=True
        ),
        lax.all_to_all(
            full_dk.astype(jnp.bfloat16), "head", split_axis=0, concat_axis=1, tiled=True
        ),
        lax.all_to_all(
            full_dv.astype(jnp.bfloat16), "head", split_axis=0, concat_axis=1, tiled=True
        ),
    )
    return (
        win_dq.astype(jnp.bfloat16),
        grads_back[0],
        grads_back[1],
        full_dq.astype(jnp.bfloat16),
        grads_back[2],
        grads_back[3],
        sink_total,
    )


def solution(mesh):
    in_specs = (
        P("ctx", "head"),
        P(("ctx", "head"), None),
        P(("ctx", "head"), None),
        P("ctx", "head"),
        P("ctx", "head"),
        P(("ctx", "head"), None),
        P(("ctx", "head"), None),
        P("ctx", "head"),
        P(None, "head"),
        P(),
    )
    out_specs = (
        P("ctx", "head"),
        P(("ctx", "head"), None),
        P(("ctx", "head"), None),
        P("ctx", "head"),
        P(("ctx", "head"), None),
        P(("ctx", "head"), None),
        P(None, "head"),
    )
    return jax.shard_map(body, mesh=mesh, in_specs=in_specs, out_specs=out_specs, check_vma=False)
```

profile of v0, /device:TPU:1, one launch (start us, length us, event | category | flops | bytes accessed | tf_op | source)
XLA Modules:
  0.0 552.3 jit_solution(17931334810956905545)
XLA Ops:
  2.0 10.1 %all-to-all-start.4 = ((bf16[32,4,128]{2,0,1:T(8,128)(2,1)}), bf16[32,4,128]{2,0,1:T(8,128)(2,1)S(1)}, u32[]{:S(2)}, u32[]{:S(2)}) async-start(bf16[32,4,128]{2,0,1:T(8,128)(2,1)} %copy_bitcast_fusion.5), calls=%async_computation.4 | async-start | bytes 65536 | tf_op jit(solution)/shard_map/all_to_all | solution.py:113
  17.8 3.3 all-to-all-start.5
  21.3 3.0 all-to-all-done.5
  24.3 4.6 all-to-all-start
  30.2 2.0 all-to-all-done
  32.2 4.6 all-to-all-start.1
  39.4 1.8 copy.144
  44.4 2.2 collective-permute-start.6
  46.6 3.3 collective-permute-start.7
  49.9 4.4 collective-permute-start.8
  57.8 5.1 collective-permute-start.9
  63.0 2.9 collective-permute-start.10
  66.1 3.5 collective-permute-start.11
  69.8 6.0 %collective-permute-start = (bf16[128,128]{1,0:T(8,128)(2,1)}, bf16[128,128]{1,0:T(8,128)(2,1)}, u32[]{:S(2)}, u32[]{:S(2)}) collective-permute-start(bf16[128,128]{1,0:T(8,128)(2,1)} %bitcast.37), channel_id=1, source_target_pairs={{0,4},{4,8},{8,12},{12,16},{16,20},{20,24},{24,28},{28,32},{32,36}... | collective-permute-start | bytes 98312 | tf_op jit(solution)/shard_map/ppermute | solution.py:18
  76.0 2.0 collective-permute-start.1
  79.9 29.0 %while.33 = (s32[]{:T(128)}, bf16[2,128,8,64]{1,3,2,0:T(8,128)(2,1)}, f32[2,640,64]{1,2,0:T(8,128)}, f32[2,640,64]{1,2,0:T(8,128)}, f32[2,8]{1,0:T(2,128)}, /*in...) while((s32[]{:T(128)}, ...), condition=%wide.region_11.12_spmd, body=%wide.region_6.11_spmd.sunk | while | flops 519355392 | bytes 23923760 | solution.py:84
  87.0 2.4 fusion.184
  89.5 1.8 fusion.181
  92.5 1.9 fusion.182
  101.5 2.4 fusion.184
  103.9 1.8 fusion.181
  107.0 1.9 fusion.182
  114.1 8.3 %while.32 = (s32[]{:T(128)}, bf16[2,128,8,64]{1,3,2,0:T(8,128)(2,1)S(1)}, f32[2,256,64]{1,2,0:T(8,128)}, f32[2,256,64]{1,2,0:T(8,128)}, f32[2,8]{1,0:T(2,128)S(1...) while((s32[]{:T(128)}, ...), condition=%wide.region_5.6_spmd, body=%wide.region_0.5_spmd.sunk | while | flops 205020160 | bytes 10725941 | solution.py:84
  136.9 314.7 %psum.7 = f32[2,16]{1,0:T(2,128)} all-reduce(f32[2,16]{1,0:T(2,128)S(1)} %pad_maximum_fusion.2), channel_id=1, replica_groups=mesh['ctx'=128,'head'=4] {'ctx'}, use_global_device_ids=true, to_apply=%region_12.13 | all-reduce | flops 32 | bytes 256 | tf_op jit(solution)/shard_map/psum | solution.py:191
  457.6 62.9 %all-to-all-start.7 = ((bf16[4,32,128]{2,1,0:T(8,128)(2,1)}), bf16[4,32,128]{2,1,0:T(8,128)(2,1)S(1)}, u32[]{:S(2)}, u32[]{:S(2)}) async-start(bf16[4,32,128]{2,1,0:T(8,128)(2,1)} %bitcast.116), calls=%async_computation.7 | async-start | bytes 65536 | tf_op jit(solution)/shard_map/all_to_all | solution.py:202
  521.9 6.2 %collective-permute-done.2 = bf16[128,128]{0,1:T(8,128)(2,1)S(1)} collective-permute-done((bf16[128,128]{0,1:T(8,128)(2,1)S(1)}, bf16[128,128]{0,1:T(8,128)(2,1)S(1)}, u32[]{:S(2)}, u32[]{:S(2)}) %collective-permute-start.2) | collective-permute-done | bytes 32800 | tf_op jit(solution)/shard_map/ppermute | solution.py:18
  530.3 3.8 all-to-all-start.6
  534.7 2.6 all-to-all-done.6
  537.3 4.0 all-to-all-start.3
  541.9 2.6 all-to-all-done.3
  544.5 4.0 all-to-all-start.2
  549.1 2.6 all-to-all-done.2
  (238 shorter events, 76.2 us)
Async XLA Ops:
  1.4 41.5 %copy-start.5 = (bf16[128,1024]{1,0:T(8,128)(2,1)S(1)}, bf16[128,1024]{1,0:T(8,128)(2,1)}, u32[]{:S(2)}) copy-start(bf16[128,1024]{1,0:T(8,128)(2,1)} %param.17) | copy-start | bytes 786436
  2.0 15.8 %all-to-all-start.4 = ((bf16[32,4,128]{2,0,1:T(8,128)(2,1)}), bf16[32,4,128]{2,0,1:T(8,128)(2,1)S(1)}, u32[]{:S(2)}, u32[]{:S(2)}) async-start(bf16[32,4,128]{2,0,1:T(8,128)(2,1)} %copy_bitcast_fusion.5), calls=%async_computation.4 | async-start | bytes 65536 | tf_op jit(solution)/shard_map/all_to_all | solution.py:113
  17.8 6.5 %all-to-all-start.5 = ((bf16[32,4,128]{2,0,1:T(8,128)(2,1)}), bf16[32,4,128]{2,0,1:T(8,128)(2,1)S(1)}, u32[]{:S(2)}, u32[]{:S(2)}) async-start(bf16[32,4,128]{2,0,1:T(8,128)(2,1)} %copy_bitcast_fusion.4), calls=%async_computation.5 | async-start | bytes 65536 | tf_op jit(solution)/shard_map/all_to_all | solution.py:114
  24.3 7.9 %all-to-all-start = ((bf16[32,4,128]{2,0,1:T(8,128)(2,1)}), bf16[32,4,128]{2,0,1:T(8,128)(2,1)}, u32[]{:S(2)}, u32[]{:S(2)}) async-start(bf16[32,4,128]{2,0,1:T(8,128)(2,1)} %copy_bitcast_fusion.7), calls=%async_computation | async-start | bytes 65536 | tf_op jit(solution)/shard_map/all_to_all | solution.py:111
  28.9 28.9 %collective-permute-start.4 = (bf16[128,128]{1,0:T(8,128)(2,1)S(1)}, bf16[128,128]{1,0:T(8,128)(2,1)S(1)}, u32[]{:S(2)}, u32[]{:S(2)}) collective-permute-start(bf16[128,128]{1,0:T(8,128)(2,1)S(1)} %bitcast.440), channel_id=1, source_target_pairs={{0,16},{4,20},{8,24},{12,28},{16,32},{20,36},{24,40},{28,44},{32,4... | collective-permute-start | bytes 98312 | tf_op jit(solution)/shard_map/ppermute | solution.py:18
  32.2 24.1 %all-to-all-start.1 = ((bf16[32,4,128]{2,0,1:T(8,128)(2,1)}), bf16[32,4,128]{2,0,1:T(8,128)(2,1)}, u32[]{:S(2)}, u32[]{:S(2)}) async-start(bf16[32,4,128]{2,0,1:T(8,128)(2,1)} %copy_bitcast_fusion.6), calls=%async_computation.1 | async-start | bytes 65536 | tf_op jit(solution)/shard_map/all_to_all | solution.py:112
  43.1 23.0 %collective-permute-start.5 = (bf16[128,128]{1,0:T(8,128)(2,1)S(1)}, bf16[128,128]{1,0:T(8,128)(2,1)S(1)}, u32[]{:S(2)}, u32[]{:S(2)}) collective-permute-start(bf16[128,128]{1,0:T(8,128)(2,1)S(1)} %bitcast.441), channel_id=1, source_target_pairs={{0,12},{4,16},{8,20},{12,24},{16,28},{20,32},{24,36},{28,40},{32,4... | collective-permute-start | bytes 98312 | tf_op jit(solution)/shard_map/ppermute | solution.py:18
  44.4 25.4 %collective-permute-start.6 = (bf16[128,128]{1,0:T(8,128)(2,1)S(1)}, bf16[128,128]{1,0:T(8,128)(2,1)S(1)}, u32[]{:S(2)}, u32[]{:S(2)}) collective-permute-start(bf16[128,128]{1,0:T(8,128)(2,1)S(1)} %bitcast.442), channel_id=1, source_target_pairs={{0,8},{4,12},{8,16},{12,20},{16,24},{20,28},{24,32},{28,36},{32,40... | collective-permute-start | bytes 98312 | tf_op jit(solution)/shard_map/ppermute | solution.py:18
  46.6 29.3 %collective-permute-start.7 = (bf16[128,128]{1,0:T(8,128)(2,1)S(1)}, bf16[128,128]{1,0:T(8,128)(2,1)S(1)}, u32[]{:S(2)}, u32[]{:S(2)}) collective-permute-start(bf16[128,128]{1,0:T(8,128)(2,1)S(1)} %bitcast.443), channel_id=1, source_target_pairs={{0,4},{4,8},{8,12},{12,16},{16,20},{20,24},{24,28},{28,32},{32,36}... | collective-permute-start | bytes 98312 | tf_op jit(solution)/shard_map/ppermute | solution.py:18
  49.9 13.1 %collective-permute-start.8 = (bf16[128,128]{1,0:T(8,128)(2,1)S(1)}, bf16[128,128]{1,0:T(8,128)(2,1)S(1)}, u32[]{:S(2)}, u32[]{:S(2)}) collective-permute-start(bf16[128,128]{1,0:T(8,128)(2,1)S(1)} %bitcast.445), channel_id=1, source_target_pairs={{0,16},{4,20},{8,24},{12,28},{16,32},{20,36},{24,40},{28,44},{32,4... | collective-permute-start | bytes 98312 | tf_op jit(solution)/shard_map/ppermute | solution.py:18
  57.8 20.3 %collective-permute-start.9 = (bf16[128,128]{1,0:T(8,128)(2,1)S(1)}, bf16[128,128]{1,0:T(8,128)(2,1)S(1)}, u32[]{:S(2)}, u32[]{:S(2)}) collective-permute-start(bf16[128,128]{1,0:T(8,128)(2,1)S(1)} %bitcast.447), channel_id=1, source_target_pairs={{0,12},{4,16},{8,20},{12,24},{16,28},{20,32},{24,36},{28,40},{32,4... | collective-permute-start | bytes 98312 | tf_op jit(solution)/shard_map/ppermute | solution.py:18
  63.0 15.2 %collective-permute-start.10 = (bf16[128,128]{1,0:T(8,128)(2,1)S(1)}, bf16[128,128]{1,0:T(8,128)(2,1)S(1)}, u32[]{:S(2)}, u32[]{:S(2)}) collective-permute-start(bf16[128,128]{1,0:T(8,128)(2,1)S(1)} %bitcast.448), channel_id=1, source_target_pairs={{0,8},{4,12},{8,16},{12,20},{16,24},{20,28},{24,32},{28,36},{32,40... | collective-permute-start | bytes 98312 | tf_op jit(solution)/shard_map/ppermute | solution.py:18
  66.1 12.3 %collective-permute-start.11 = (bf16[128,128]{1,0:T(8,128)(2,1)S(1)}, bf16[128,128]{1,0:T(8,128)(2,1)S(1)}, u32[]{:S(2)}, u32[]{:S(2)}) collective-permute-start(bf16[128,128]{1,0:T(8,128)(2,1)S(1)} %bitcast.449), channel_id=1, source_target_pairs={{0,4},{4,8},{8,12},{12,16},{16,20},{20,24},{24,28},{28,32},{32,36}... | collective-permute-start | bytes 98312 | tf_op jit(solution)/shard_map/ppermute | solution.py:18
  69.8 41.7 %collective-permute-start = (bf16[128,128]{1,0:T(8,128)(2,1)}, bf16[128,128]{1,0:T(8,128)(2,1)}, u32[]{:S(2)}, u32[]{:S(2)}) collective-permute-start(bf16[128,128]{1,0:T(8,128)(2,1)} %bitcast.37), channel_id=1, source_target_pairs={{0,4},{4,8},{8,12},{12,16},{16,20},{20,24},{24,28},{28,32},{32,36}... | collective-permute-start | bytes 98312 | tf_op jit(solution)/shard_map/ppermute | solution.py:18
  76.0 36.4 %collective-permute-start.1 = (bf16[128,128]{1,0:T(8,128)(2,1)}, bf16[128,128]{1,0:T(8,128)(2,1)}, u32[]{:S(2)}, u32[]{:S(2)}) collective-permute-start(bf16[128,128]{1,0:T(8,128)(2,1)} %bitcast.44), channel_id=1, source_target_pairs={{0,4},{4,8},{8,12},{12,16},{16,20},{20,24},{24,28},{28,32},{32,36}... | collective-permute-start | bytes 98312 | tf_op jit(solution)/shard_map/ppermute | solution.py:18
  91.3 3.1 copy-start.2
  105.8 3.1 copy-start.2
  105.8 3.1 copy-start.17
  122.5 329.1 %collective-permute-start.16 = (bf16[128,128]{0,1:T(8,128)(2,1)S(1)}, bf16[128,128]{0,1:T(8,128)(2,1)S(1)}, u32[]{:S(2)}, u32[]{:S(2)}) collective-permute-start(bf16[128,128]{0,1:T(8,128)(2,1)S(1)} %bitcast.472), channel_id=1, source_target_pairs={{4,0},{8,4},{12,8},{16,12},{20,16},{24,20},{28,24},{32,28},{36,32}... | collective-permute-start | bytes 98312 | tf_op jit(solution)/shard_map/ppermute | solution.py:18
  123.8 329.1 %collective-permute-start.17 = (bf16[128,128]{0,1:T(8,128)(2,1)S(1)}, bf16[128,128]{0,1:T(8,128)(2,1)S(1)}, u32[]{:S(2)}, u32[]{:S(2)}) collective-permute-start(bf16[128,128]{0,1:T(8,128)(2,1)S(1)} %bitcast.471), channel_id=1, source_target_pairs={{8,0},{12,4},{16,8},{20,12},{24,16},{28,20},{32,24},{36,28},{40,32... | collective-permute-start | bytes 98312 | tf_op jit(solution)/shard_map/ppermute | solution.py:18
  125.1 329.1 %collective-permute-start.18 = (bf16[128,128]{0,1:T(8,128)(2,1)S(1)}, bf16[128,128]{0,1:T(8,128)(2,1)S(1)}, u32[]{:S(2)}, u32[]{:S(2)}) collective-permute-start(bf16[128,128]{0,1:T(8,128)(2,1)S(1)} %bitcast.470), channel_id=1, source_target_pairs={{12,0},{16,4},{20,8},{24,12},{28,16},{32,20},{36,24},{40,28},{44,3... | collective-permute-start | bytes 98312 | tf_op jit(solution)/shard_map/ppermute | solution.py:18
  126.4 329.1 %collective-permute-start.19 = (bf16[128,128]{0,1:T(8,128)(2,1)S(1)}, bf16[128,128]{0,1:T(8,128)(2,1)S(1)}, u32[]{:S(2)}, u32[]{:S(2)}) collective-permute-start(bf16[128,128]{0,1:T(8,128)(2,1)S(1)} %bitcast.468), channel_id=1, source_target_pairs={{16,0},{20,4},{24,8},{28,12},{32,16},{36,20},{40,24},{44,28},{48,3... | collective-permute-start | bytes 98312 | tf_op jit(solution)/shard_map/ppermute | solution.py:18
  128.7 391.8 %collective-permute-start.12 = (bf16[128,128]{0,1:T(8,128)(2,1)S(1)}, bf16[128,128]{0,1:T(8,128)(2,1)S(1)}, u32[]{:S(2)}, u32[]{:S(2)}) collective-permute-start(bf16[128,128]{0,1:T(8,128)(2,1)S(1)} %bitcast.469), channel_id=1, source_target_pairs={{4,0},{8,4},{12,8},{16,12},{20,16},{24,20},{28,24},{32,28},{36,32}... | collective-permute-start | bytes 98312 | tf_op jit(solution)/shard_map/ppermute | solution.py:18
  451.6 70.2 %collective-permute-start.13 = (bf16[128,128]{0,1:T(8,128)(2,1)S(1)}, bf16[128,128]{0,1:T(8,128)(2,1)S(1)}, u32[]{:S(2)}, u32[]{:S(2)}) collective-permute-start(bf16[128,128]{0,1:T(8,128)(2,1)S(1)} %bitcast.467), channel_id=1, source_target_pairs={{8,0},{12,4},{16,8},{20,12},{24,16},{28,20},{32,24},{36,28},{40,32... | collective-permute-start | bytes 98312 | tf_op jit(solution)/shard_map/ppermute | solution.py:18
  452.9 68.9 %collective-permute-start.14 = (bf16[128,128]{0,1:T(8,128)(2,1)S(1)}, bf16[128,128]{0,1:T(8,128)(2,1)S(1)}, u32[]{:S(2)}, u32[]{:S(2)}) collective-permute-start(bf16[128,128]{0,1:T(8,128)(2,1)S(1)} %bitcast.466), channel_id=1, source_target_pairs={{12,0},{16,4},{20,8},{24,12},{28,16},{32,20},{36,24},{40,28},{44,3... | collective-permute-start | bytes 98312 | tf_op jit(solution)/shard_map/ppermute | solution.py:18
  454.2 67.6 %collective-permute-start.15 = (bf16[128,128]{0,1:T(8,128)(2,1)S(1)}, bf16[128,128]{0,1:T(8,128)(2,1)S(1)}, u32[]{:S(2)}, u32[]{:S(2)}) collective-permute-start(bf16[128,128]{0,1:T(8,128)(2,1)S(1)} %bitcast.465), channel_id=1, source_target_pairs={{16,0},{20,4},{24,8},{28,12},{32,16},{36,20},{40,24},{44,28},{48,3... | collective-permute-start | bytes 98312 | tf_op jit(solution)/shard_map/ppermute | solution.py:18
  455.5 66.4 %collective-permute-start.3 = (bf16[128,128]{0,1:T(8,128)(2,1)S(1)}, bf16[128,128]{0,1:T(8,128)(2,1)S(1)}, u32[]{:S(2)}, u32[]{:S(2)}) collective-permute-start(bf16[128,128]{0,1:T(8,128)(2,1)S(1)} %bitcast.464), channel_id=1, source_target_pairs={{4,0},{8,4},{12,8},{16,12},{20,16},{24,20},{28,24},{32,28},{36,32}... | collective-permute-start | bytes 98312 | tf_op jit(solution)/shard_map/ppermute | solution.py:18
  457.6 72.7 %all-to-all-start.7 = ((bf16[4,32,128]{2,1,0:T(8,128)(2,1)}), bf16[4,32,128]{2,1,0:T(8,128)(2,1)S(1)}, u32[]{:S(2)}, u32[]{:S(2)}) async-start(bf16[4,32,128]{2,1,0:T(8,128)(2,1)} %bitcast.116), calls=%async_computation.7 | async-start | bytes 65536 | tf_op jit(solution)/shard_map/all_to_all | solution.py:202
  520.5 7.6 %collective-permute-start.2 = (bf16[128,128]{0,1:T(8,128)(2,1)S(1)}, bf16[128,128]{0,1:T(8,128)(2,1)S(1)}, u32[]{:S(2)}, u32[]{:S(2)}) collective-permute-start(bf16[128,128]{0,1:T(8,128)(2,1)S(1)} %bitcast.463), channel_id=1, source_target_pairs={{4,0},{8,4},{12,8},{16,12},{20,16},{24,20},{28,24},{32,28},{36,32}... | collective-permute-start | bytes 98312 | tf_op jit(solution)/shard_map/ppermute | solution.py:18
  530.3 7.0 %all-to-all-start.6 = ((bf16[4,32,128]{2,1,0:T(8,128)(2,1)}), bf16[4,32,128]{2,1,0:T(8,128)(2,1)S(1)}, u32[]{:S(2)}, u32[]{:S(2)}) async-start(bf16[4,32,128]{2,1,0:T(8,128)(2,1)} %bitcast.104), calls=%async_computation.6 | async-start | bytes 65536 | tf_op jit(solution)/shard_map/all_to_all | solution.py:199
  537.3 7.2 %all-to-all-start.3 = ((bf16[4,32,128]{2,1,0:T(8,128)(2,1)}), bf16[4,32,128]{2,1,0:T(8,128)(2,1)S(1)}, u32[]{:S(2)}, u32[]{:S(2)}) async-start(bf16[4,32,128]{2,1,0:T(8,128)(2,1)} %bitcast.62), calls=%async_computation.3 | async-start | bytes 65536 | tf_op jit(solution)/shard_map/all_to_all | solution.py:196
  544.5 7.2 %all-to-all-start.2 = ((bf16[4,32,128]{2,1,0:T(8,128)(2,1)}), bf16[4,32,128]{2,1,0:T(8,128)(2,1)S(1)}, u32[]{:S(2)}, u32[]{:S(2)}) async-start(bf16[4,32,128]{2,1,0:T(8,128)(2,1)} %bitcast.56), calls=%async_computation.2 | async-start | bytes 65536 | tf_op jit(solution)/shard_map/all_to_all | solution.py:193
  (32 other events, 51.1 us)
where the time goes:
time: 563 us; the launch traced here: 552 us
  blocking collectives  315 us (56%)
  starting transfers between devices  142 us (25%)
  local copies, waits for them, and re-layouts  41.5 us (7%)
  matrix products  24.4 us (4%)
  waiting for transfers between devices  18.9 us (3%)
  other arithmetic  8.8 us (2%)
    psum x1, blocking collectives, body(): sink_total = lax.psum(jnp.stack([win_dsink, full_dsink]), 'ctx')  315 us
    all_to_all x1, starting transfers between devices, body(): lax.all_to_all(full_dv.astype(jnp.bfloat16), 'head', split_axis=0, concat...  62.9 us
    ppermute x20, starting transfers between devices, passed_along(): return lax.ppermute(shard, axis, pairs)  44.9 us
  transfers between devices with their start and end apart: 28, of which 6 were waited for; matrix products, arithmetic and copies ran while one was open for 11% of the time, Pallas kernels for 0%

commit v1 on v0

v1 whole, which is shorter than its diff:
```python
import jax
import jax.numpy as jnp
from jax import lax
from jax.experimental import pallas as pl
from jax.experimental.pallas import tpu as pltpu
from jax.sharding import PartitionSpec as P

HEAD_DIM = 64
CYCLE = 4
BLOCK = 128
PAIRS = 4
NEG = -1e30
VMEM = pl.BlockSpec(memory_space=pltpu.VMEM)
SMEM = pl.BlockSpec(memory_space=pltpu.SMEM)
BF16, F32 = jnp.bfloat16, jnp.float32


def passed_along(shard, axis, by):
    size = lax.axis_size(axis)
    pairs = [(i, i + by) for i in range(size) if 0 <= i + by < size]
    return lax.ppermute(shard, axis, pairs)


def low_lanes(rows):
    return lax.broadcasted_iota(jnp.int32, (rows, 128), 1) < 64


def both_ways(tile):
    turned = pltpu.roll(tile, 64, 1)
    low = low_lanes(tile.shape[0])
    return jnp.where(low, tile, turned), jnp.where(low, turned, tile)


def pair_rows(tile):
    low = low_lanes(128)
    zero = jnp.zeros_like(tile)
    return jnp.concatenate([jnp.where(low, tile, zero), jnp.where(low, zero, tile)], axis=0)


def dot(a, b, contract):
    return lax.dot_general(a, b, (contract, ((), ())), preferred_element_type=F32)


def build_bias(bias, seg_ref, me, blocks, windowed):
    seg_q = jnp.broadcast_to(seg_ref[pl.ds(me, 1), :], (128, 128))
    key_row = lax.broadcasted_iota(jnp.int32, (128, 128), 0)
    query_col = lax.broadcasted_iota(jnp.int32, (128, 128), 1)
    for b in range(blocks):
        lag = blocks - 1 - b
        at = me - lag
        seg_row = jnp.broadcast_to(seg_ref[pl.ds(jnp.maximum(at, 0), 1), :], (128, 128))
        seg_k = jnp.transpose(seg_row.astype(F32)).astype(jnp.int32)
        allowed = (seg_k == seg_q) & (at >= 0)
        if lag == 0:
            allowed = allowed & (key_row <= query_col)
        elif windowed:
            allowed = allowed & (key_row > query_col)
        tile = jnp.where(allowed, 0.0, NEG).astype(F32)
        bias[b * 128 : (b + 1) * 128, :] = jnp.concatenate([tile, tile], axis=1)


def layer(layer_id, sinks_ref, q_ref, do_ref, keys, values, bias, kd, vd, kt, ws, dss, dq_ref, sink_acc):
    blocks = len(keys)
    rows = blocks * 128
    for b in range(blocks):
        span = slice(b * 128, (b + 1) * 128)
        key = keys[b]().astype(F32) * (HEAD_DIM**-0.5)
        k0, k1 = both_ways(key)
        kd[0, span, :] = k0.astype(BF16)
        kd[1, span, :] = k1.astype(BF16)
        turned = jnp.transpose(key).astype(BF16)
        kt[0, :, span] = turned[:64]
        kt[1, :, span] = turned[64:]
        v0, v1 = both_ways(values[b]().astype(F32))
        vd[0, span, :] = v0.astype(BF16)
        vd[1, span, :] = v1.astype(BF16)
    lane = lax.broadcasted_iota(jnp.int32, (1, 256), 1)
    sums = []
    for g in range(2):
        q2s, do2s = [], []
        for j in range(PAIRS):
            p = g * PAIRS + j
            q2 = pair_rows(q_ref[:, p * 128 : (p + 1) * 128])
            do2 = pair_rows(do_ref[:, p * 128 : (p + 1) * 128])
            q2s.append(q2)
            do2s.append(do2)
            sink = jnp.where(lane < 128, sinks_ref[layer_id, 2 * p], sinks_ref[layer_id, 2 * p + 1])
            s = dot(kd[g, :rows, :], q2, ((1,), (1,))) + bias[:rows, :]
            m = jnp.maximum(jnp.max(s, axis=0, keepdims=True), sink)
            e = jnp.exp(s - m)
            sink_term = jnp.exp(sink - m)
            inverse = 1.0 / (jnp.sum(e, axis=0, keepdims=True) + sink_term)
            pr = e * inverse
            dp = dot(vd[g, :rows, :], do2, ((1,), (1,)))
            delta = jnp.sum(pr * dp, axis=0, keepdims=True)
            ws[:rows, j * 256 : (j + 1) * 256] = pr.astype(BF16)
            dss[:rows, j * 256 : (j + 1) * 256] = (pr * (dp - delta)).astype(BF16)
            grad = -(sink_term * inverse) * delta
            at = layer_id * 16 + 2 * p
            sink_acc[at : at + 1, :] = grad[:, :128]
            sink_acc[at + 1 : at + 2, :] = grad[:, 128:]
        q_all = jnp.concatenate(q2s, axis=0)
        do_all = jnp.concatenate(do2s, axis=0)
        dk = dot(dss[:rows, :], q_all, ((1,), (0,)))
        dv = dot(ws[:rows, :], do_all, ((1,), (0,)))
        sums.append((dk + pltpu.roll(dk, 64, 1), dv + pltpu.roll(dv, 64, 1)))
        dqt = dot(kt[g, :, :rows], dss[:rows, :], ((1,), (0,)))
        for j in range(PAIRS):
            p = g * PAIRS + j
            both = jnp.concatenate([dqt[:, j * 256 : j * 256 + 128], dqt[:, j * 256 + 128 : j * 256 + 256]], axis=0)
            dq_ref[:, p * 128 : (p + 1) * 128] = jnp.transpose(both).astype(BF16)
    low = low_lanes(rows)
    dk = jnp.where(low, sums[0][0], sums[1][0]) * (HEAD_DIM**-0.5)
    dv = jnp.where(low, sums[0][1], sums[1][1])
    return dk, dv


def attention_kernel(
    me_ref, sinks_ref, seg_ref, wq_ref, wdo_ref, fq_ref, fdo_ref, own, far1, far2, far3, far4,
    wdq_ref, fdq_ref, mine, back1, back2, back3, back4, sink_ref,
    bias, kd, vd, kt, ws, dss, sink_acc,
):
    me = me_ref[0]
    sink_acc[...] = jnp.zeros_like(sink_acc)

    def tile(ref, at):
        return lambda: ref[:, at : at + 128]

    build_bias(bias, seg_ref, me, 2, True)
    dk, dv = layer(
        0, sinks_ref, wq_ref, wdo_ref, [tile(far1, 0), tile(own, 0)], [tile(far1, 128), tile(own, 128)],
        bias, kd, vd, kt, ws, dss, wdq_ref, sink_acc,
    )
    back1[:, 0:128] = dk[:128].astype(BF16)
    back1[:, 128:256] = dv[:128].astype(BF16)
    mine[:, 0:128] = dk[128:]
    mine[:, 128:256] = dv[128:]
    build_bias(bias, seg_ref, me, CYCLE + 1, False)
    dk, dv = layer(
        1, sinks_ref, fq_ref, fdo_ref,
        [tile(far4, 0), tile(far3, 0), tile(far2, 0), tile(far1, 256), tile(own, 256)],
        [tile(far4, 128), tile(far3, 128), tile(far2, 128), tile(far1, 384), tile(own, 384)],
        bias, kd, vd, kt, ws, dss, fdq_ref, sink_acc,
    )
    for b, ref in enumerate((back4, back3, back2)):
        ref[:, 0:128] = dk[b * 128 : (b + 1) * 128].astype(BF16)
        ref[:, 128:256] = dv[b * 128 : (b + 1) * 128].astype(BF16)
    back1[:, 256:384] = dk[384:512].astype(BF16)
    back1[:, 384:512] = dv[384:512].astype(BF16)
    mine[:, 256:384] = dk[512:]
    mine[:, 384:512] = dv[512:]
    total = jnp.sum(jnp.transpose(sink_acc[...]), axis=0, keepdims=True)
    sink_ref[...] = jnp.broadcast_to(total, sink_ref.shape)


def attention(me, sinks, seg, wq, wdo, fq, fdo, own, far1, far2, far3, far4):
    rows = (CYCLE + 1) * 128
    shape = jax.ShapeDtypeStruct
    return pl.pallas_call(
        attention_kernel,
        out_shape=(
            shape((128, 1024), BF16), shape((128, 1024), BF16), shape((128, 512), F32), shape((128, 512), BF16),
            shape((128, 256), BF16), shape((128, 256), BF16), shape((128, 256), BF16), shape((128, 128), F32),
        ),
        in_specs=[SMEM, SMEM] + [VMEM] * 10,
        out_specs=[VMEM] * 8,
        scratch_shapes=[
            pltpu.VMEM((rows, 256), F32),
            pltpu.VMEM((2, rows, 128), BF16),
            pltpu.VMEM((2, rows, 128), BF16),
            pltpu.VMEM((2, 64, rows), BF16),
            pltpu.VMEM((rows, 1024), BF16),
            pltpu.VMEM((rows, 1024), BF16),
            pltpu.VMEM((128, 128), F32),
        ],
        compiler_params=pltpu.CompilerParams(vmem_limit_bytes=40 << 20),
        cost_estimate=pl.CostEstimate(flops=3_000_000_000, bytes_accessed=4_000_000, transcendentals=2_000_000),
    )(me, sinks, seg, wq, wdo, fq, fdo, own, far1, far2, far3, far4)


def pack_kernel(wk, wv, fk, fv, out):
    for a, ref in enumerate((wk, wv, fk, fv)):
        for t in range(4):
            out[t * 32 : (t + 1) * 32, a * 128 : (a + 1) * 128] = ref[:, t * 128 : (t + 1) * 128]


def sum_kernel(mine, back1, back2, back3, back4, out):
    out[:, :256] = (mine[:, :256] + back1[:, :256].astype(F32)).astype(BF16)
    banded = back2[...].astype(F32) + back3[...].astype(F32) + back4[...].astype(F32)
    out[:, 256:] = (mine[:, 256:] + back1[:, 256:].astype(F32) + banded).astype(BF16)


def unpack_kernel(grads, sink_terms, wk, wv, fk, fv, sinks):
    for a, ref in enumerate((wk, wv, fk, fv)):
        for t in range(4):
            ref[:, t * 128 : (t + 1) * 128] = grads[t * 32 : (t + 1) * 32, a * 128 : (a + 1) * 128]
    total = jnp.sum(sink_terms[...], axis=0, keepdims=True)
    sinks[0:1, :] = total[:, 0:16]
    sinks[1:2, :] = total[:, 16:32]


def local_call(kernel, out_shape, args):
    return pl.pallas_call(
        kernel,
        out_shape=out_shape,
        in_specs=[VMEM] * len(args),
        out_specs=jax.tree.map(lambda _: VMEM, out_shape),
        compiler_params=pltpu.CompilerParams(vmem_limit_bytes=4 << 20),
        cost_estimate=pl.CostEstimate(flops=100_000, bytes_accessed=500_000, transcendentals=0),
    )(*args)


def body(win_q, win_k, win_v, win_dout, full_q, full_k, full_v, full_dout, sinks, segments):
    shape = jax.ShapeDtypeStruct
    packed = local_call(pack_kernel, shape((128, 512), BF16), (win_k, win_v, full_k, full_v))
    own = lax.all_to_all(packed, "head", split_axis=0, concat_axis=0, tiled=True)
    banded = own[:, 256:]
    far1 = passed_along(own, "ctx", 1)
    far2, far3, far4 = (passed_along(banded, "ctx", by) for by in (2, 3, 4))
    me = lax.axis_index("ctx").astype(jnp.int32).reshape(1)
    win_dq, full_dq, mine, back1, back2, back3, back4, sink_rows = attention(
        me, sinks, segments.reshape(128, 128), win_q, win_dout, full_q, full_dout, own, far1, far2, far3, far4
    )
    sink_terms = lax.all_to_all(sink_rows, "ctx", split_axis=0, concat_axis=0, tiled=True)
    backs = [passed_along(back, "ctx", -by) for by, back in enumerate((back1, back2, back3, back4), 1)]
    summed = local_call(sum_kernel, shape((128, 512), BF16), (mine, *backs))
    grads = lax.all_to_all(summed, "head", split_axis=0, concat_axis=0, tiled=True)
    slices = (shape((32, 512), BF16),) * 4
    win_dk, win_dv, full_dk, full_dv, sink_grads = local_call(
        unpack_kernel, slices + (shape((2, 16), F32),), (grads, sink_terms)
    )
    return win_dq, win_dk, win_dv, full_dq, full_dk, full_dv, sink_grads


def solution(mesh):
    in_specs = (
        P("ctx", "head"),
        P(("ctx", "head"), None),
        P(("ctx", "head"), None),
        P("ctx", "head"),
        P("ctx", "head"),
        P(("ctx", "head"), None),
        P(("ctx", "head"), None),
        P("ctx", "head"),
        P(None, "head"),
        P(),
    )
    out_specs = (
        P("ctx", "head"),
        P(("ctx", "head"), None),
        P(("ctx", "head"), None),
        P("ctx", "head"),
        P(("ctx", "head"), None),
        P(("ctx", "head"), None),
        P(None, "head"),
    )
    return jax.shard_map(body, mesh=mesh, in_specs=in_specs, out_specs=out_specs, check_vma=False)
```

time: 563 us -> 109 us (0.19); the launches traced: 552 us -> 108 us
  blocking collectives: 315 us -> 65.3 us
  starting transfers between devices: 142 us -> 15.4 us
  local copies, waits for them, and re-layouts: 41.5 us -> 5.6 us
  matrix products: 24.4 us -> 0 us
  Pallas kernels: 0 us -> 8.8 us
  other arithmetic: 8.8 us -> 0 us
  waiting for transfers between devices: 18.9 us -> 12 us
    psum x1 -> x0, blocking collectives: 315 us -> none  [body(): sink_total = lax.psum(jnp.stack([win_dsink, full_dsink]), 'ctx')]
    all_to_all x8 -> x0, starting transfers between devices: 97.4 us -> none  [the longest x1 62.9 us: body(): lax.all_to_all(full_dv.astype(jnp.bfloat16), 'head', split_axis=0, concat...]
    all_to_all x0 -> x3, blocking collectives: none -> 65.3 us  [the longest x1 42.2 us: body(): lax.all_to_all(sink_rows, 'ctx', split_axis=0, concat_axis=0, tiled=True)]
    ppermute x20 -> x8, starting transfers between devices: 44.9 us -> 15.4 us  [passed_along(): return lax.ppermute(shard, axis, pairs)]
    dot_general x24 -> x0, matrix products: 24.4 us -> none  [the longest x4 5.42 us: block_grads(): jnp.einsum('gqk,qgd->kd', weights, cotangent, preferred_element_type=jnp....]
    all_to_all x8 -> x0, waiting for transfers between devices: 12.7 us -> none  [the longest x1 3 us: body(): lax.all_to_all(full_v, 'head', split_axis=1, concat_axis=0, tiled=True)]
    pallas_call x0 -> x4, Pallas kernels: none -> 8.8 us  [the longest x1 8.05 us: attention(): pl.pallas_call(attention_kernel, out_shape=(shape((128, 1024), BF16), sha...]
    all_to_all x8 -> x0, local copies, waits for them, and re-layouts: 7.22 us -> none  [the longest x1 1.38 us: body(): lax.all_to_all(full_v, 'head', split_axis=1, concat_axis=0, tiled=True)]
  transfers between devices with their start and end apart: 28 -> 8, of which waited for: 6 -> 4; matrix products, arithmetic and copies ran while one was open for 11% -> 0% of each run, Pallas kernels for 0% -> 0%
where the time goes in v1:
time: 109 us; the launch traced here: 108 us
  blocking collectives  65.3 us (60%)
  starting transfers between devices  15.4 us (14%)
  waiting for transfers between devices  12 us (11%)
  Pallas kernels  8.8 us (8%)
  local copies, waits for them, and re-layouts  5.6 us (5%)
    all_to_all x1, blocking collectives, body(): lax.all_to_all(sink_rows, 'ctx', split_axis=0, concat_axis=0, tiled=True)  42.2 us
    ppermute x8, starting transfers between devices, passed_along(): return lax.ppermute(shard, axis, pairs)  15.4 us
    all_to_all x1, blocking collectives, body(): lax.all_to_all(packed, 'head', split_axis=0, concat_axis=0, tiled=True)  13 us
    ppermute x8, waiting for transfers between devices, passed_along(): return lax.ppermute(shard, axis, pairs)  12 us
    all_to_all x1, blocking collectives, body(): lax.all_to_all(summed, 'head', split_axis=0, concat_axis=0, tiled=True)  10.2 us
    pallas_call x1, Pallas kernels, attention(): pl.pallas_call(attention_kernel, out_shape=(shape((128, 1024), BF16), sha...  8.05 us
    unnamed x20, local copies, waits for them, and re-layouts  5.6 us
  transfers between devices with their start and end apart: 8, of which 4 were waited for; matrix products, arithmetic and copies ran while one was open for 0% of the time, Pallas kernels for 0%

profile of v1, /device:TPU:1, one launch (start us, length us, event | category | flops | bytes accessed | tf_op | source)
XLA Modules:
  0.0 107.9 jit_solution(12521942647678242239)
XLA Ops:
  0.6 0.0 copy-start
  0.6 0.7 copy-done
  1.4 0.8 copy-done.1
  2.2 0.8 copy-done.2
  2.9 0.8 copy-done.3
  3.7 0.0 copy-start.4
  3.7 13.0 %all_to_all.33 = bf16[4,32,512]{2,1,0:T(8,128)(2,1)S(1)} all-to-all(bf16[4,32,512]{2,1,0:T(8,128)(2,1)S(1)} %bitcast.11), channel_id=1, replica_groups=mesh['ctx'=128,'head'=4] {'head'}, dimensions={0} | all-to-all | bytes 262144 | tf_op jit(solution)/shard_map/all_to_all | solution.py:216
  16.7 1.4 %collective-permute-start = (bf16[128,512]{1,0:T(8,128)(2,1)S(1)}, bf16[128,512]{1,0:T(8,128)(2,1)S(1)}, u32[]{:S(2)}, u32[]{:S(2)}) collective-permute-start(bf16[128,512]{1,0:T(8,128)(2,1)S(1)} %bitcast.13), channel_id=1, source_target_pairs={{0,4},{4,8},{8,12},{12,16},{16,20},{20,24},{24,28},{28,32},{32,36}... | collective-permute-start | bytes 393224 | tf_op jit(solution)/shard_map/ppermute | solution.py:21
  18.1 2.8 %collective-permute-start.3 = (bf16[128,256]{1,0:T(8,128)(2,1)S(1)}, bf16[128,256]{1,0:T(8,128)(2,1)S(1)}, u32[]{:S(2)}, u32[]{:S(2)}) collective-permute-start(bf16[128,256]{1,0:T(8,128)(2,1)S(1)} %slice.4), channel_id=1, source_target_pairs={{0,16},{4,20},{8,24},{12,28},{16,32},{20,36},{24,40},{28,44},{32,4... | collective-permute-start | bytes 196616 | tf_op jit(solution)/shard_map/ppermute | solution.py:21
  20.9 3.5 %collective-permute-start.2 = (bf16[128,256]{1,0:T(8,128)(2,1)S(1)}, bf16[128,256]{1,0:T(8,128)(2,1)S(1)}, u32[]{:S(2)}, u32[]{:S(2)}) collective-permute-start(bf16[128,256]{1,0:T(8,128)(2,1)S(1)} %slice.4), channel_id=1, source_target_pairs={{0,12},{4,16},{8,20},{12,24},{16,28},{20,32},{24,36},{28,40},{32,4... | collective-permute-start | bytes 196616 | tf_op jit(solution)/shard_map/ppermute | solution.py:21
  24.5 2.5 %collective-permute-start.1 = (bf16[128,256]{1,0:T(8,128)(2,1)S(1)}, bf16[128,256]{1,0:T(8,128)(2,1)S(1)}, u32[]{:S(2)}, u32[]{:S(2)}) collective-permute-start(bf16[128,256]{1,0:T(8,128)(2,1)S(1)} %slice.4), channel_id=1, source_target_pairs={{0,8},{4,12},{8,16},{12,20},{16,24},{20,28},{24,32},{28,36},{32,40... | collective-permute-start | bytes 196616 | tf_op jit(solution)/shard_map/ppermute | solution.py:21
  27.0 0.0 collective-permute-done.3.far4
  27.0 0.0 collective-permute-done.2.far3
  27.0 1.4 %collective-permute-done.1.far2 = bf16[128,256]{1,0:T(8,128)(2,1)S(1)} collective-permute-done((bf16[128,256]{1,0:T(8,128)(2,1)S(1)}, bf16[128,256]{1,0:T(8,128)(2,1)S(1)}, u32[]{:S(2)}, u32[]{:S(2)}) %collective-permute-start.1) | collective-permute-done | bytes 65568 | tf_op jit(solution)/shard_map/ppermute | solution.py:21
  28.4 0.0 collective-permute-done.far1
  28.4 0.0 copy-done.5
  28.5 0.7 copy-done.9
  29.1 0.9 copy-done.6
  30.1 0.9 copy-done.7
  31.0 8.1 %shard_map.154 = (bf16[128,1024]{1,0:T(8,128)(2,1)}, bf16[128,1024]{1,0:T(8,128)(2,1)}, f32[128,512]{1,0:T(8,128)S(1)}, bf16[128,512]{1,0:T(8,128)(2,1)S(1)}, bf...) custom-call(s32[1]{0:T(128)} %bitcast.me_ref, ...), custom_call_target="tpu_custom_call" | custom-call | flops 3000000000 | bytes 4000000 | tf_op jit(solution)/shard_map/pallas_call | solution.py:159
  39.1 1.3 %collective-permute-start.4 = (bf16[128,512]{1,0:T(8,128)(2,1)S(1)}, bf16[128,512]{1,0:T(8,128)(2,1)S(1)}, u32[]{:S(2)}, u32[]{:S(2)}) collective-permute-start(bf16[128,512]{1,0:T(8,128)(2,1)S(1)} %get-tuple-element.22), channel_id=1, source_target_pairs={{4,0},{8,4},{12,8},{16,12},{20,16},{24,20},{28,24},{32,28},{36,32}... | collective-permute-start | bytes 393224 | tf_op jit(solution)/shard_map/ppermute | solution.py:21
  40.4 1.3 %collective-permute-start.5 = (bf16[128,256]{1,0:T(8,128)(2,1)S(1)}, bf16[128,256]{1,0:T(8,128)(2,1)S(1)}, u32[]{:S(2)}, u32[]{:S(2)}) collective-permute-start(bf16[128,256]{1,0:T(8,128)(2,1)S(1)} %get-tuple-element.23), channel_id=1, source_target_pairs={{8,0},{12,4},{16,8},{20,12},{24,16},{28,20},{32,24},{36,28},{40,32... | collective-permute-start | bytes 196616 | tf_op jit(solution)/shard_map/ppermute | solution.py:21
  41.7 1.3 %collective-permute-start.6 = (bf16[128,256]{1,0:T(8,128)(2,1)S(1)}, bf16[128,256]{1,0:T(8,128)(2,1)S(1)}, u32[]{:S(2)}, u32[]{:S(2)}) collective-permute-start(bf16[128,256]{1,0:T(8,128)(2,1)S(1)} %get-tuple-element.24), channel_id=1, source_target_pairs={{12,0},{16,4},{20,8},{24,12},{28,16},{32,20},{36,24},{40,28},{44,3... | collective-permute-start | bytes 196616 | tf_op jit(solution)/shard_map/ppermute | solution.py:21
  43.0 1.3 %collective-permute-start.7 = (bf16[128,256]{1,0:T(8,128)(2,1)S(1)}, bf16[128,256]{1,0:T(8,128)(2,1)S(1)}, u32[]{:S(2)}, u32[]{:S(2)}) collective-permute-start(bf16[128,256]{1,0:T(8,128)(2,1)S(1)} %get-tuple-element.25), channel_id=1, source_target_pairs={{16,0},{20,4},{24,8},{28,12},{32,16},{36,20},{40,24},{44,28},{48,3... | collective-permute-start | bytes 196616 | tf_op jit(solution)/shard_map/ppermute | solution.py:21
  44.3 4.9 %collective-permute-done.5.back2 = bf16[128,256]{1,0:T(8,128)(2,1)S(1)} collective-permute-done((bf16[128,256]{1,0:T(8,128)(2,1)S(1)}, bf16[128,256]{1,0:T(8,128)(2,1)S(1)}, u32[]{:S(2)}, u32[]{:S(2)}) %collective-permute-start.5) | collective-permute-done | bytes 65568 | tf_op jit(solution)/shard_map/ppermute | solution.py:21
  49.1 2.0 %collective-permute-done.6.back3 = bf16[128,256]{1,0:T(8,128)(2,1)S(1)} collective-permute-done((bf16[128,256]{1,0:T(8,128)(2,1)S(1)}, bf16[128,256]{1,0:T(8,128)(2,1)S(1)}, u32[]{:S(2)}, u32[]{:S(2)}) %collective-permute-start.6) | collective-permute-done | bytes 65568 | tf_op jit(solution)/shard_map/ppermute | solution.py:21
  51.1 3.7 %collective-permute-done.7.back4 = bf16[128,256]{1,0:T(8,128)(2,1)S(1)} collective-permute-done((bf16[128,256]{1,0:T(8,128)(2,1)S(1)}, bf16[128,256]{1,0:T(8,128)(2,1)S(1)}, u32[]{:S(2)}, u32[]{:S(2)}) %collective-permute-start.7) | collective-permute-done | bytes 65568 | tf_op jit(solution)/shard_map/ppermute | solution.py:21
  54.8 0.0 collective-permute-done.4.back1
  54.8 0.1 shard_map.155
  54.9 10.2 %all_to_all.34 = bf16[4,32,512]{2,1,0:T(8,128)(2,1)S(1)} all-to-all(bf16[4,32,512]{2,1,0:T(8,128)(2,1)S(1)} %bitcast.12), channel_id=1, replica_groups=mesh['ctx'=128,'head'=4] {'head'}, dimensions={0} | all-to-all | bytes 262144 | tf_op jit(solution)/shard_map/all_to_all | solution.py:227
  65.0 42.2 %all_to_all.35 = f32[128,1,128]{2,1,0:T(1,128)S(1)} all-to-all(f32[128,1,128]{2,1,0:T(1,128)S(1)} %bitcast.17), channel_id=1, replica_groups=mesh['ctx'=128,'head'=4] {'ctx'}, dimensions={0} | all-to-all | bytes 131072 | tf_op jit(solution)/shard_map/all_to_all | solution.py:224
  107.2 0.7 shard_map.156
  (12 shorter events, 0.0 us)
Async XLA Ops:
  0.6 0.8 copy-start
  1.4 0.8 copy-start.1
  2.2 0.8 copy-start.2
  2.9 0.8 copy-start.3
  3.7 24.8 %copy-start.5 = (bf16[128,1024]{1,0:T(8,128)(2,1)S(1)}, bf16[128,1024]{1,0:T(8,128)(2,1)}, u32[]{:S(2)}) copy-start(bf16[128,1024]{1,0:T(8,128)(2,1)} %wdo_ref.1) | copy-start | bytes 786436
  3.7 24.7 %copy-start.4 = (bf16[128,1024]{1,0:T(8,128)(2,1)S(1)}, bf16[128,1024]{1,0:T(8,128)(2,1)}, u32[]{:S(2)}) copy-start(bf16[128,1024]{1,0:T(8,128)(2,1)} %wq_ref.1) | copy-start | bytes 786436
  16.7 11.7 %copy-start.8 = (s32[16384]{0:T(1024)S(1)}, s32[16384]{0:T(1024)}, u32[]{:S(2)}) copy-start(s32[16384]{0:T(1024)} %param.19) | copy-start | bytes 196612
  16.7 11.7 %collective-permute-start = (bf16[128,512]{1,0:T(8,128)(2,1)S(1)}, bf16[128,512]{1,0:T(8,128)(2,1)S(1)}, u32[]{:S(2)}, u32[]{:S(2)}) collective-permute-start(bf16[128,512]{1,0:T(8,128)(2,1)S(1)} %bitcast.13), channel_id=1, source_target_pairs={{0,4},{4,8},{8,12},{12,16},{16,20},{20,24},{24,28},{28,32},{32,36}... | collective-permute-start | bytes 393224 | tf_op jit(solution)/shard_map/ppermute | solution.py:21
  18.1 8.9 %collective-permute-start.3 = (bf16[128,256]{1,0:T(8,128)(2,1)S(1)}, bf16[128,256]{1,0:T(8,128)(2,1)S(1)}, u32[]{:S(2)}, u32[]{:S(2)}) collective-permute-start(bf16[128,256]{1,0:T(8,128)(2,1)S(1)} %slice.4), channel_id=1, source_target_pairs={{0,16},{4,20},{8,24},{12,28},{16,32},{20,36},{24,40},{28,44},{32,4... | collective-permute-start | bytes 196616 | tf_op jit(solution)/shard_map/ppermute | solution.py:21
  20.9 6.1 %collective-permute-start.2 = (bf16[128,256]{1,0:T(8,128)(2,1)S(1)}, bf16[128,256]{1,0:T(8,128)(2,1)S(1)}, u32[]{:S(2)}, u32[]{:S(2)}) collective-permute-start(bf16[128,256]{1,0:T(8,128)(2,1)S(1)} %slice.4), channel_id=1, source_target_pairs={{0,12},{4,16},{8,20},{12,24},{16,28},{20,32},{24,36},{28,40},{32,4... | collective-permute-start | bytes 196616 | tf_op jit(solution)/shard_map/ppermute | solution.py:21
  24.5 4.0 %collective-permute-start.1 = (bf16[128,256]{1,0:T(8,128)(2,1)S(1)}, bf16[128,256]{1,0:T(8,128)(2,1)S(1)}, u32[]{:S(2)}, u32[]{:S(2)}) collective-permute-start(bf16[128,256]{1,0:T(8,128)(2,1)S(1)} %slice.4), channel_id=1, source_target_pairs={{0,8},{4,12},{8,16},{12,20},{16,24},{20,28},{24,32},{28,36},{32,40... | collective-permute-start | bytes 196616 | tf_op jit(solution)/shard_map/ppermute | solution.py:21
  28.4 0.7 copy-start.9
  29.1 0.9 copy-start.6
  30.1 0.9 copy-start.7
  39.1 15.8 %collective-permute-start.4 = (bf16[128,512]{1,0:T(8,128)(2,1)S(1)}, bf16[128,512]{1,0:T(8,128)(2,1)S(1)}, u32[]{:S(2)}, u32[]{:S(2)}) collective-permute-start(bf16[128,512]{1,0:T(8,128)(2,1)S(1)} %get-tuple-element.22), channel_id=1, source_target_pairs={{4,0},{8,4},{12,8},{16,12},{20,16},{24,20},{28,24},{32,28},{36,32}... | collective-permute-start | bytes 393224 | tf_op jit(solution)/shard_map/ppermute | solution.py:21
  40.4 8.8 %collective-permute-start.5 = (bf16[128,256]{1,0:T(8,128)(2,1)S(1)}, bf16[128,256]{1,0:T(8,128)(2,1)S(1)}, u32[]{:S(2)}, u32[]{:S(2)}) collective-permute-start(bf16[128,256]{1,0:T(8,128)(2,1)S(1)} %get-tuple-element.23), channel_id=1, source_target_pairs={{8,0},{12,4},{16,8},{20,12},{24,16},{28,20},{32,24},{36,28},{40,32... | collective-permute-start | bytes 196616 | tf_op jit(solution)/shard_map/ppermute | solution.py:21
  41.7 9.5 %collective-permute-start.6 = (bf16[128,256]{1,0:T(8,128)(2,1)S(1)}, bf16[128,256]{1,0:T(8,128)(2,1)S(1)}, u32[]{:S(2)}, u32[]{:S(2)}) collective-permute-start(bf16[128,256]{1,0:T(8,128)(2,1)S(1)} %get-tuple-element.24), channel_id=1, source_target_pairs={{12,0},{16,4},{20,8},{24,12},{28,16},{32,20},{36,24},{40,28},{44,3... | collective-permute-start | bytes 196616 | tf_op jit(solution)/shard_map/ppermute | solution.py:21
  43.0 11.9 %collective-permute-start.7 = (bf16[128,256]{1,0:T(8,128)(2,1)S(1)}, bf16[128,256]{1,0:T(8,128)(2,1)S(1)}, u32[]{:S(2)}, u32[]{:S(2)}) collective-permute-start(bf16[128,256]{1,0:T(8,128)(2,1)S(1)} %get-tuple-element.25), channel_id=1, source_target_pairs={{16,0},{20,4},{24,8},{28,12},{32,16},{36,20},{40,24},{44,28},{48,3... | collective-permute-start | bytes 196616 | tf_op jit(solution)/shard_map/ppermute | solution.py:21

commit v2 on v1

v2 whole, which is shorter than its diff:
```python
import jax
import jax.numpy as jnp
from jax import lax
from jax.experimental import pallas as pl
from jax.experimental.pallas import tpu as pltpu
from jax.sharding import PartitionSpec as P

HEAD_DIM = 64
CYCLE = 4
BLOCK = 128
PAIRS = 4
NEG = -1e30
PAIRS_OF_BLOCKS = 64
CHUNK = 48
VMEM = pl.BlockSpec(memory_space=pltpu.VMEM)
SMEM = pl.BlockSpec(memory_space=pltpu.SMEM)
ANY = pl.BlockSpec(memory_space=pl.ANY)
HBM = pl.BlockSpec(memory_space=pltpu.HBM)
BF16, F32 = jnp.bfloat16, jnp.float32


def passed_along(shard, axis, by):
    size = lax.axis_size(axis)
    pairs = [(i, i + by) for i in range(size) if 0 <= i + by < size]
    return lax.ppermute(shard, axis, pairs)


def low_lanes(rows):
    return lax.broadcasted_iota(jnp.int32, (rows, 128), 1) < 64


def both_ways(tile):
    turned = pltpu.roll(tile, 64, 1)
    low = low_lanes(tile.shape[0])
    return jnp.where(low, tile, turned), jnp.where(low, turned, tile)


def pair_rows(tile):
    low = low_lanes(128)
    zero = jnp.zeros_like(tile)
    return jnp.concatenate([jnp.where(low, tile, zero), jnp.where(low, zero, tile)], axis=0)


def dot(a, b, contract):
    return lax.dot_general(a, b, (contract, ((), ())), preferred_element_type=F32)


def build_bias(bias, seg_ref, me, blocks, windowed):
    seg_q = jnp.broadcast_to(seg_ref[pl.ds(me, 1), :], (128, 128))
    key_row = lax.broadcasted_iota(jnp.int32, (128, 128), 0)
    query_col = lax.broadcasted_iota(jnp.int32, (128, 128), 1)
    for b in range(blocks):
        lag = blocks - 1 - b
        at = me - lag
        seg_row = jnp.broadcast_to(seg_ref[pl.ds(jnp.maximum(at, 0), 1), :], (128, 128))
        seg_k = jnp.transpose(seg_row.astype(F32)).astype(jnp.int32)
        allowed = (seg_k == seg_q) & (at >= 0)
        if lag == 0:
            allowed = allowed & (key_row <= query_col)
        elif windowed:
            allowed = allowed & (key_row > query_col)
        tile = jnp.where(allowed, 0.0, NEG).astype(F32)
        bias[b * 128 : (b + 1) * 128, :] = jnp.concatenate([tile, tile], axis=1)


def layer(layer_id, sinks_ref, q_ref, do_ref, odd, places, bias, kd, vd, kt, ws, dss, dq_ref, sink_acc, dq_hbm, sems):
    blocks = len(places) - 1
    rows = blocks * 128

    def block(b, shift):
        first, second = (
            ref[row : row + 128, col + shift : col + shift + 128].astype(F32) for ref, row, col in places[b : b + 2]
        )
        return jnp.where(odd, second, first)

    for b in range(blocks):
        span = slice(b * 128, (b + 1) * 128)
        key = block(b, 0) * (HEAD_DIM**-0.5)
        k0, k1 = both_ways(key)
        kd[0, span, :] = k0.astype(BF16)
        kd[1, span, :] = k1.astype(BF16)
        turned = jnp.transpose(key).astype(BF16)
        kt[0, :, span] = turned[:64]
        kt[1, :, span] = turned[64:]
        v0, v1 = both_ways(block(b, 128))
        vd[0, span, :] = v0.astype(BF16)
        vd[1, span, :] = v1.astype(BF16)
    lane = lax.broadcasted_iota(jnp.int32, (1, 256), 1)
    sums, sends = [], []
    for g in range(2):
        q2s, do2s = [], []
        for j in range(PAIRS):
            p = g * PAIRS + j
            q2 = pair_rows(q_ref[:, p * 128 : (p + 1) * 128])
            do2 = pair_rows(do_ref[:, p * 128 : (p + 1) * 128])
            q2s.append(q2)
            do2s.append(do2)
            sink = jnp.where(lane < 128, sinks_ref[layer_id : layer_id + 1, 2 * p : 2 * p + 1], sinks_ref[layer_id : layer_id + 1, 2 * p + 1 : 2 * p + 2])
            s = dot(kd[g, :rows, :], q2, ((1,), (1,))) + bias[:rows, :]
            m = jnp.maximum(jnp.max(s, axis=0, keepdims=True), sink)
            e = jnp.exp(s - m)
            sink_term = jnp.exp(sink - m)
            inverse = 1.0 / (jnp.sum(e, axis=0, keepdims=True) + sink_term)
            pr = e * inverse
            dp = dot(vd[g, :rows, :], do2, ((1,), (1,)))
            delta = jnp.sum(pr * dp, axis=0, keepdims=True)
            ws[:rows, j * 256 : (j + 1) * 256] = pr.astype(BF16)
            dss[:rows, j * 256 : (j + 1) * 256] = (pr * (dp - delta)).astype(BF16)
            grad = -(sink_term * inverse) * delta
            at = layer_id * 16 + 2 * p
            sink_acc[at : at + 1, :] = grad[:, :128]
            sink_acc[at + 1 : at + 2, :] = grad[:, 128:]
        q_all = jnp.concatenate(q2s, axis=0)
        do_all = jnp.concatenate(do2s, axis=0)
        dk = dot(dss[:rows, :], q_all, ((1,), (0,)))
        dv = dot(ws[:rows, :], do_all, ((1,), (0,)))
        sums.append((dk + pltpu.roll(dk, 64, 1), dv + pltpu.roll(dv, 64, 1)))
        dqt = dot(kt[g, :, :rows], dss[:rows, :], ((1,), (0,)))
        for j in range(PAIRS):
            p = g * PAIRS + j
            both = jnp.concatenate([dqt[:, j * 256 : j * 256 + 128], dqt[:, j * 256 + 128 : j * 256 + 256]], axis=0)
            dq_ref[:, p * 128 : (p + 1) * 128] = jnp.transpose(both).astype(BF16)
        cols = slice(g * 512, (g + 1) * 512)
        sends.append(pltpu.make_async_copy(dq_ref.at[:, cols], dq_hbm.at[:, cols], sems.at[1 + g]))
        sends[-1].start()
    low = low_lanes(rows)
    dk = jnp.where(low, sums[0][0], sums[1][0]) * (HEAD_DIM**-0.5)
    dv = jnp.where(low, sums[0][1], sums[1][1])
    for send in sends:
        send.wait()
    return dk, dv


def shifted(grad, blocks, odd):
    zero = jnp.zeros((128, 128), F32)
    parts = [zero] + [grad[b * 128 : (b + 1) * 128] for b in range(blocks)] + [zero]
    return [jnp.where(odd, parts[b], parts[b + 1]) for b in range(blocks + 1)]


def window_kernel(
    me_ref, sinks_hbm, seg_ref, q_ref, do_ref, own, far2,
    dq_hbm, mine, back, sinks_ref, band_bias, sink_acc,
    bias, kd, vd, kt, ws, dss, dq_ref, sems,
):
    me, odd = me_ref[0], me_ref[1] == 1
    fetch = pltpu.make_async_copy(sinks_hbm, sinks_ref, sems.at[0])
    fetch.start()
    sink_acc[...] = jnp.zeros_like(sink_acc)
    build_bias(bias, seg_ref, me, 2, True)
    build_bias(band_bias, seg_ref, me, CYCLE + 1, False)
    fetch.wait()
    blocks = [(far2, 256, 0), (own, 0, 0), (own, 128, 0)]
    dk, dv = layer(
        0, sinks_ref, q_ref, do_ref, odd, blocks, bias, kd, vd, kt, ws, dss, dq_ref, sink_acc, dq_hbm, sems
    )
    for at, grad in ((0, dk), (128, dv)):
        parts = shifted(grad, 2, odd)
        back[:, at : at + 128] = parts[0].astype(BF16)
        mine[:128, at : at + 128] = parts[1]
        mine[128:, at : at + 128] = parts[2]


def band_kernel(
    me_ref, sinks_ref, bias, q_ref, do_ref, own, far2, far4, win_back, win_acc,
    dq_hbm, mine, back2, back4, sink_ref,
    kd, vd, kt, ws, dss, dq_ref, sink_acc, sems,
):
    odd = me_ref[1] == 1
    sink_acc[...] = win_acc[...]
    blocks = [(far4, 0, 0), (far4, 128, 0), (far2, 0, 0), (far2, 128, 0), (own, 0, 256), (own, 128, 256)]
    dk, dv = layer(
        1, sinks_ref, q_ref, do_ref, odd, blocks, bias, kd, vd, kt, ws, dss, dq_ref, sink_acc, dq_hbm, sems
    )
    for at, grad in ((0, dk), (128, dv)):
        parts = shifted(grad, CYCLE + 1, odd)
        for half in range(2):
            rows = slice(half * 128, (half + 1) * 128)
            back4[rows, at : at + 128] = parts[half].astype(BF16)
            back2[rows, at : at + 128] = parts[2 + half].astype(BF16)
            mine[rows, at : at + 128] = parts[4 + half]
    back2[256:, :] = win_back[...]
    total = jnp.sum(jnp.transpose(sink_acc[...]), axis=0, keepdims=True)
    row = lax.broadcasted_iota(jnp.int32, sink_ref.shape, 0)
    sink_ref[...] = jnp.where(row % 2 == 0, total, 0.0)


def scratch(rows):
    return [
        pltpu.VMEM((2, rows, 128), BF16),
        pltpu.VMEM((2, rows, 128), BF16),
        pltpu.VMEM((2, 64, rows), BF16),
        pltpu.VMEM((rows, 1024), BF16),
        pltpu.VMEM((rows, 1024), BF16),
        pltpu.VMEM((128, 1024), BF16),
    ]


def window_call(me, sinks, seg, q, do, own, far2):
    shape = jax.ShapeDtypeStruct
    return pl.pallas_call(
        window_kernel,
        out_shape=(
            shape((128, 1024), BF16), shape((256, 256), F32), shape((128, 256), BF16),
            shape((2, 16), F32), shape(((CYCLE + 1) * 128, 256), F32), shape((128, 128), F32),
        ),
        in_specs=[SMEM, HBM] + [VMEM] * 5,
        out_specs=[HBM] + [VMEM] * 5,
        scratch_shapes=[pltpu.VMEM((256, 256), F32)] + scratch(256) + [pltpu.SemaphoreType.DMA((3,))],
        compiler_params=pltpu.CompilerParams(vmem_limit_bytes=14 << 20),
        cost_estimate=pl.CostEstimate(flops=2_000_000_000, bytes_accessed=1_000_000, transcendentals=500_000),
    )(me, sinks, seg, q, do, own, far2)


def band_call(me, sinks, bias, q, do, own, far2, far4, win_back, win_acc):
    shape = jax.ShapeDtypeStruct
    return pl.pallas_call(
        band_kernel,
        out_shape=(
            shape((128, 1024), BF16), shape((256, 256), F32), shape((384, 256), BF16), shape((256, 256), BF16),
            shape((PAIRS_OF_BLOCKS * 2, 128), F32),
        ),
        in_specs=[SMEM] + [VMEM] * 9,
        out_specs=[HBM] + [VMEM] * 4,
        scratch_shapes=scratch((CYCLE + 1) * 128) + [pltpu.VMEM((128, 128), F32), pltpu.SemaphoreType.DMA((3,))],
        compiler_params=pltpu.CompilerParams(vmem_limit_bytes=24 << 20),
        cost_estimate=pl.CostEstimate(flops=5_000_000_000, bytes_accessed=2_000_000, transcendentals=1_500_000),
    )(me, sinks, bias, q, do, own, far2, far4, win_back, win_acc)


def pack_kernel(wk, wv, fk, fv, out, held, sems):
    copies = [pltpu.make_async_copy(ref, held.at[a], sems.at[a]) for a, ref in enumerate((wk, wv, fk, fv))]
    for copy in copies:
        copy.start()
    for a, copy in enumerate(copies):
        copy.wait()
        for t in range(8):
            h = t % 4
            out[t * 32 : (t + 1) * 32, a * 128 : (a + 1) * 128] = held[a, :, h * 128 : (h + 1) * 128]


def three_parts(row):
    high = row.astype(BF16).astype(F32)
    middle = (row - high).astype(BF16).astype(F32)
    low = row - high - middle
    at = lax.broadcasted_iota(jnp.int32, (16, 128), 0)
    rest = jnp.where(at == 2, low, 0.0)
    return jnp.where(at == 0, high, jnp.where(at == 1, middle, rest)).astype(BF16)


def sum_kernel(win_mine, band_mine, back2, back4, sink_terms, out):
    win = [win_mine[:128, :], win_mine[128:, :] + back2[256:, :].astype(F32)]
    sinks = three_parts(jnp.sum(sink_terms[...], axis=0, keepdims=True))
    for half in range(2):
        rows = slice(half * 128, (half + 1) * 128)
        band = (band_mine[rows, :] + back2[rows, :].astype(F32) + back4[rows, :].astype(F32)).astype(BF16)
        for t in range(4):
            at = (half * 4 + t) * CHUNK
            out[at : at + 32, :256] = win[half][t * 32 : (t + 1) * 32].astype(BF16)
            out[at : at + 32, 256:] = band[t * 32 : (t + 1) * 32]
            out[at + 32 : at + 48, :128] = sinks
            out[at + 32 : at + 48, 128:] = jnp.zeros((16, 384), BF16)


def unpack_kernel(me_ref, grads, wk, wv, fk, fv, sinks):
    def chunk(yh, t):
        at = (yh * 4 + t) * CHUNK
        return grads[at : at + 32, :].astype(F32)

    for t in range(4):
        total = (chunk(0, t) + chunk(1, t)).astype(BF16)
        for a, ref in enumerate((wk, wv, fk, fv)):
            ref[:, t * 128 : (t + 1) * 128] = total[:, a * 128 : (a + 1) * 128]
    parts = jnp.zeros((16, 128), F32)
    for yh in range(2):
        at = pl.multiple_of((yh * 4 + me_ref[2]) * CHUNK + 32, 16)
        parts = parts + grads[pl.ds(at, 16), :128].astype(F32)
    total = jnp.sum(parts, axis=0, keepdims=True)
    sinks[0:1, :] = total[:, 0:16]
    sinks[1:2, :] = total[:, 16:32]


def local_call(kernel, out_shape, args, in_specs, scratch_shapes=(), flops=100_000, vmem=4):
    return pl.pallas_call(
        kernel,
        out_shape=out_shape,
        in_specs=in_specs,
        out_specs=jax.tree.map(lambda _: VMEM, out_shape),
        scratch_shapes=scratch_shapes,
        compiler_params=pltpu.CompilerParams(vmem_limit_bytes=vmem << 20),
        cost_estimate=pl.CostEstimate(flops=flops, bytes_accessed=500_000, transcendentals=0),
    )(*args)


def body(win_q, win_k, win_v, win_dout, full_q, full_k, full_v, full_dout, sinks, segments):
    shape = jax.ShapeDtypeStruct
    held = [pltpu.VMEM((4, 32, 512), BF16), pltpu.SemaphoreType.DMA((4,))]
    packed = local_call(pack_kernel, shape((256, 512), BF16), (win_k, win_v, full_k, full_v), [HBM] * 4, held, vmem=60)
    own = lax.all_to_all(packed, ("yh", "head"), split_axis=0, concat_axis=0, tiled=True)
    banded = own[:, 256:]
    far2 = passed_along(jnp.concatenate([banded, own[128:, :256]], axis=0), "pair", 1)
    far4 = passed_along(banded, "pair", 2)
    pair, yh, head = (lax.axis_index(axis).astype(jnp.int32) for axis in ("pair", "yh", "head"))
    me = jnp.stack([pair * 2 + yh, yh, head])
    win_dq, win_mine, win_back, sink_vals, bias, win_acc = window_call(
        me, sinks, segments.reshape(128, 128), win_q, win_dout, own, far2
    )
    full_dq, band_mine, back2, back4, sink_rows = band_call(
        me, sink_vals, bias, full_q, full_dout, own, far2, far4, win_back, win_acc
    )
    back2, back4 = passed_along(back2, "pair", -1), passed_along(back4, "pair", -2)
    sink_terms = lax.all_to_all(sink_rows, "pair", split_axis=0, concat_axis=0, tiled=True)
    summed = local_call(
        sum_kernel, shape((8 * CHUNK, 512), BF16), (win_mine, band_mine, back2, back4, sink_terms), [VMEM] * 5
    )
    grads = lax.all_to_all(summed, ("yh", "head"), split_axis=0, concat_axis=0, tiled=True)
    win_dk, win_dv, full_dk, full_dv, sink_grads = local_call(
        unpack_kernel, (shape((32, 512), BF16),) * 4 + (shape((2, 16), F32),), (me, grads), [SMEM, VMEM]
    )
    return win_dq, win_dk, win_dv, full_dq, full_dk, full_dv, sink_grads


def solution(mesh):
    mesh = jax.sharding.Mesh(mesh.devices.reshape(PAIRS_OF_BLOCKS, 2, 4), ("pair", "yh", "head"))
    tokens = P(("pair", "yh"), "head")
    slices = P(("pair", "yh", "head"), None)
    in_specs = (tokens, slices, slices, tokens, tokens, slices, slices, tokens, P(None, "head"), P())
    out_specs = (tokens, slices, slices, tokens, slices, slices, P(None, "head"))
    return jax.shard_map(body, mesh=mesh, in_specs=in_specs, out_specs=out_specs, check_vma=False)
```

time: 109 us -> 82.8 us (0.76)
  blocking collectives: 65.3 us -> 31.8 us
  starting transfers between devices: 15.4 us -> 23.5 us
  local copies, waits for them, and re-layouts: 5.6 us -> 0.05 us
  Pallas kernels: 8.8 us -> 13.4 us
    all_to_all x3 -> x2, blocking collectives: 65.3 us -> 31.8 us  [the longest x1 16.7 us: body(): lax.all_to_all(packed, ('yh', 'head'), split_axis=0, concat_axis=0, tiled...]
    all_to_all x0 -> x1, starting transfers between devices: none -> 17.4 us  [body(): lax.all_to_all(sink_rows, 'pair', split_axis=0, concat_axis=0, tiled=True)]
    ppermute x8 -> x4, starting transfers between devices: 15.4 us -> 6.1 us  [passed_along(): return lax.ppermute(shard, axis, pairs)]
    unnamed x20 -> x12, local copies, waits for them, and re-layouts: 5.6 us -> 0.03 us
    all_to_all x0 -> x1, waiting for transfers between devices: none -> 4.65 us  [body(): lax.all_to_all(sink_rows, 'pair', split_axis=0, concat_axis=0, tiled=True)]
    pallas_call x4 -> x5, Pallas kernels: 8.8 us -> 13.4 us  [the longest x1 6.88 us: band_call(): pl.pallas_call(band_kernel, out_shape=(shape((128, 1024), BF16), shape((2...]
    ppermute x8 -> x4, waiting for transfers between devices: 12 us -> 8.03 us  [passed_along(): return lax.ppermute(shard, axis, pairs)]
  transfers between devices with their start and end apart: 8 -> 5, of which waited for: 4 -> 3; matrix products, arithmetic and copies ran while one was open for 0% -> 0% of each run, Pallas kernels for 0% -> 4%
where the time goes in v2:
time: 82.8 us; the launch traced here: 82.4 us
  blocking collectives  31.8 us (38%)
  starting transfers between devices  23.5 us (28%)
  Pallas kernels  13.4 us (16%)
  waiting for transfers between devices  12.7 us (15%)
    all_to_all x1, starting transfers between devices, body(): lax.all_to_all(sink_rows, 'pair', split_axis=0, concat_axis=0, tiled=True)  17.4 us
    all_to_all x1, blocking collectives, body(): lax.all_to_all(packed, ('yh', 'head'), split_axis=0, concat_axis=0, tiled...  16.7 us
    all_to_all x1, blocking collectives, body(): lax.all_to_all(summed, ('yh', 'head'), split_axis=0, concat_axis=0, tiled...  15.1 us
    ppermute x4, waiting for transfers between devices, passed_along(): return lax.ppermute(shard, axis, pairs)  8.03 us
    pallas_call x1, Pallas kernels, band_call(): pl.pallas_call(band_kernel, out_shape=(shape((128, 1024), BF16), shape((2...  6.88 us
    ppermute x4, starting transfers between devices, passed_along(): return lax.ppermute(shard, axis, pairs)  6.1 us
    all_to_all x1, waiting for transfers between devices, body(): lax.all_to_all(sink_rows, 'pair', split_axis=0, concat_axis=0, tiled=True)  4.65 us
    pallas_call x1, Pallas kernels, window_call(): pl.pallas_call(window_kernel, out_shape=(shape((128, 1024), BF16), shape(...  3.69 us
  transfers between devices with their start and end apart: 5, of which 3 were waited for; matrix products, arithmetic and copies ran while one was open for 0% of the time, Pallas kernels for 4%

profile of v2, /device:TPU:1, one launch (start us, length us, event | category | flops | bytes accessed | tf_op | source)
XLA Modules:
  0.0 82.4 jit_solution(4938421973070378634)
XLA Ops:
  0.6 1.6 %shard_map.153 = bf16[256,512]{1,0:T(8,128)(2,1)} custom-call(bf16[32,512]{1,0:T(8,128)(2,1)} %wk.1, bf16[32,512]{1,0:T(8,128)(2,1)} %wv.1, bf16[32,512]{1,0:T(8,128)(2,1)} %fk.1, bf16[32,512]{1,0:T(8,128)(2,1)} %fv.1), custom_call_target="tpu_custom_call" | custom-call | flops 100000 | bytes 500000 | tf_op jit(solution)/shard_map/pallas_call | solution.py:283
  2.2 16.7 %all_to_all.33 = bf16[8,32,512]{2,1,0:T(8,128)(2,1)S(1)} all-to-all(bf16[8,32,512]{2,1,0:T(8,128)(2,1)} %bitcast.18), channel_id=1, replica_groups=mesh['pair'=64,'yh'=2,'head'=4] {'yh','head'}, dimensions={0} | all-to-all | bytes 524288 | tf_op jit(solution)/shard_map/all_to_all | solution.py:298
  18.9 0.0 copy-start.1
  18.9 0.0 copy-start
  18.9 0.0 copy-start.4
  19.0 1.4 %collective-permute-start = (bf16[384,256]{1,0:T(8,128)(2,1)S(1)}, bf16[384,256]{1,0:T(8,128)(2,1)S(1)}, u32[]{:S(2)}, u32[]{:S(2)}) collective-permute-start(bf16[384,256]{1,0:T(8,128)(2,1)S(1)} %pad_maximum_fusion), channel_id=1, source_target_pairs={{0,8},{8,16},{16,24},{24,32},{32,40},{40,48},{48,56},{56,64},{64,7... | collective-permute-start | bytes 589832 | tf_op jit(solution)/shard_map/ppermute | solution.py:25
  20.4 0.1 pad_add_fusion.me_ref
  20.5 0.0 copy-start.5
  20.5 2.1 %collective-permute-start.1 = (bf16[256,256]{1,0:T(8,128)(2,1)S(1)}, bf16[256,256]{1,0:T(8,128)(2,1)S(1)}, u32[]{:S(2)}, u32[]{:S(2)}) collective-permute-start(bf16[256,256]{1,0:T(8,128)(2,1)S(1)} %slice.8), channel_id=1, source_target_pairs={{0,16},{8,24},{16,32},{24,40},{32,48},{40,56},{48,64},{56,72},{64,... | collective-permute-start | bytes 393224 | tf_op jit(solution)/shard_map/ppermute | solution.py:25
  22.6 1.3 %collective-permute-done.far2 = bf16[384,256]{1,0:T(8,128)(2,1)S(1)} collective-permute-done((bf16[384,256]{1,0:T(8,128)(2,1)S(1)}, bf16[384,256]{1,0:T(8,128)(2,1)S(1)}, u32[]{:S(2)}, u32[]{:S(2)}) %collective-permute-start) | collective-permute-done | bytes 196640 | tf_op jit(solution)/shard_map/ppermute | solution.py:25
  23.9 0.0 copy-done.1
  23.9 0.0 copy-done
  23.9 0.0 copy-done.4
  23.9 0.0 copy-done.5
  23.9 0.0 copy-start.2
  23.9 0.0 copy-start.3
  23.9 3.7 %shard_map.154 = (bf16[128,1024]{1,0:T(8,128)(2,1)}, f32[256,256]{1,0:T(8,128)S(1)}, bf16[128,256]{1,0:T(8,128)(2,1)S(1)}, f32[2,16]{1,0:T(2,128)S(1)}, f32[640,256]{1,0:T(8,128)S(1)}, /*index=5*/f32[128,128]{1,0:T(8,128)S(1)}) custom-call(s32[3]{0:T(128)S(1)} %pad_add_fusion.me_ref, f32[2,16]{1,0:T(2,128)S(1)} %copy-done.5, s32[128,128]{1,0:T(8,128)S(1)} %bitcast.17, ...), custom_call_target="tpu_custom_call" | custom-call | flops 2000000000 | bytes 1000000 | tf_op jit(solution)/shard_map/pallas_call | solution.py:200
  27.6 0.0 collective-permute-done.1.far4
  27.6 0.0 copy-done.2
  27.6 0.0 copy-done.3
  27.6 6.9 %shard_map.155 = (bf16[128,1024]{1,0:T(8,128)(2,1)}, f32[256,256]{1,0:T(8,128)S(1)}, bf16[384,256]{1,0:T(8,128)(2,1)S(1)}, bf16[256,256]{1,0:T(8,128)(2,1)S(1)}, f32[128,128]{1,0:T(8,128)}) custom-call(s32[3]{0:T(128)S(1)} %pad_add_fusion.me_ref, f32[2,16]{1,0:T(2,128)S(1)} %get-tuple-element.25.sinks_ref, f32[640,256]{1,0:T(8,128)S(1)} %get-tuple-element.26.bias, ...), custom_call_target="tpu_custom_call" | custom-call | flops 5000000000 | bytes 2000000 | tf_op jit(solution)/shard_map/pallas_call | solution.py:216
  34.5 17.4 %all-to-all-start.1 = ((f32[64,2,128]{2,1,0:T(2,128)}), f32[64,2,128]{2,1,0:T(2,128)S(1)}, u32[]{:S(2)}, u32[]{:S(2)}) async-start(f32[64,2,128]{2,1,0:T(2,128)} %bitcast.6), calls=%async_computation.1 | async-start | bytes 131072 | tf_op jit(solution)/shard_map/all_to_all | solution.py:311
  52.0 1.3 %collective-permute-start.2 = (bf16[384,256]{1,0:T(8,128)(2,1)S(1)}, bf16[384,256]{1,0:T(8,128)(2,1)S(1)}, u32[]{:S(2)}, u32[]{:S(2)}) collective-permute-start(bf16[384,256]{1,0:T(8,128)(2,1)S(1)} %get-tuple-element.30), channel_id=1, source_target_pairs={{8,0},{16,8},{24,16},{32,24},{40,32},{48,40},{56,48},{64,56},{72,6... | collective-permute-start | bytes 589832 | tf_op jit(solution)/shard_map/ppermute | solution.py:25
  53.2 1.3 %collective-permute-start.3 = (bf16[256,256]{1,0:T(8,128)(2,1)S(1)}, bf16[256,256]{1,0:T(8,128)(2,1)S(1)}, u32[]{:S(2)}, u32[]{:S(2)}) collective-permute-start(bf16[256,256]{1,0:T(8,128)(2,1)S(1)} %get-tuple-element.31), channel_id=1, source_target_pairs={{16,0},{24,8},{32,16},{40,24},{48,32},{56,40},{64,48},{72,56},{80,... | collective-permute-start | bytes 393224 | tf_op jit(solution)/shard_map/ppermute | solution.py:25
  54.5 6.8 %collective-permute-done.3.back4 = bf16[256,256]{1,0:T(8,128)(2,1)S(1)} collective-permute-done((bf16[256,256]{1,0:T(8,128)(2,1)S(1)}, bf16[256,256]{1,0:T(8,128)(2,1)S(1)}, u32[]{:S(2)}, u32[]{:S(2)}) %collective-permute-start.3) | collective-permute-done | bytes 131104 | tf_op jit(solution)/shard_map/ppermute | solution.py:25
  61.3 0.0 collective-permute-done.2.back2
  61.3 4.7 %all-to-all-done.1 = f32[64,2,128]{2,1,0:T(2,128)S(1)} async-done(((f32[64,2,128]{2,1,0:T(2,128)}), f32[64,2,128]{2,1,0:T(2,128)S(1)}, u32[]{:S(2)}, u32[]{:S(2)}) %all-to-all-start.1) | async-done | bytes 65568 | tf_op jit(solution)/shard_map/all_to_all | solution.py:311
  66.0 0.1 shard_map.156
  66.0 15.1 %all_to_all.34 = bf16[8,48,512]{2,1,0:T(8,128)(2,1)S(1)} all-to-all(bf16[8,48,512]{2,1,0:T(8,128)(2,1)S(1)} %bitcast.11), channel_id=1, replica_groups=mesh['pair'=64,'yh'=2,'head'=4] {'yh','head'}, dimensions={0} | all-to-all | bytes 786432 | tf_op jit(solution)/shard_map/all_to_all | solution.py:315
  81.1 1.2 %shard_map.157 = (bf16[32,512]{1,0:T(8,128)(2,1)}, bf16[32,512]{1,0:T(8,128)(2,1)}, bf16[32,512]{1,0:T(8,128)(2,1)}, bf16[32,512]{1,0:T(8,128)(2,1)}, f32[2,16]{1,0:T(2,128)}) custom-call(s32[3]{0:T(128)S(1)} %pad_add_fusion.me_ref, bf16[384,512]{1,0:T(8,128)(2,1)S(1)} %bitcast.10), custom_call_target="tpu_custom_call" | custom-call | flops 100000 | bytes 500000 | tf_op jit(solution)/shard_map/pallas_call | solution.py:283
  (3 shorter events, 0.0 us)
Async XLA Ops:
  18.9 5.0 %copy-start.1 = (bf16[128,1024]{1,0:T(8,128)(2,1)S(1)}, bf16[128,1024]{1,0:T(8,128)(2,1)}, u32[]{:S(2)}) copy-start(bf16[128,1024]{1,0:T(8,128)(2,1)} %do_ref.2) | copy-start | bytes 786436
  18.9 4.9 %copy-start = (bf16[128,1024]{1,0:T(8,128)(2,1)S(1)}, bf16[128,1024]{1,0:T(8,128)(2,1)}, u32[]{:S(2)}) copy-start(bf16[128,1024]{1,0:T(8,128)(2,1)} %q_ref.2) | copy-start | bytes 786436
  18.9 4.9 %copy-start.4 = (s32[16384]{0:T(1024)S(1)}, s32[16384]{0:T(1024)}, u32[]{:S(2)}) copy-start(s32[16384]{0:T(1024)} %param.19) | copy-start | bytes 196612
  19.0 4.9 %collective-permute-start = (bf16[384,256]{1,0:T(8,128)(2,1)S(1)}, bf16[384,256]{1,0:T(8,128)(2,1)S(1)}, u32[]{:S(2)}, u32[]{:S(2)}) collective-permute-start(bf16[384,256]{1,0:T(8,128)(2,1)S(1)} %pad_maximum_fusion), channel_id=1, source_target_pairs={{0,8},{8,16},{16,24},{24,32},{32,40},{40,48},{48,56},{56,64},{64,7... | collective-permute-start | bytes 589832 | tf_op jit(solution)/shard_map/ppermute | solution.py:25
  20.5 3.4 %copy-start.5 = (f32[2,16]{1,0:T(2,128)S(1)}, f32[2,16]{1,0:T(2,128)}, u32[]{:S(2)}) copy-start(f32[2,16]{1,0:T(2,128)} %sinks_hbm.1) | copy-start | bytes 388
  20.5 7.1 %collective-permute-start.1 = (bf16[256,256]{1,0:T(8,128)(2,1)S(1)}, bf16[256,256]{1,0:T(8,128)(2,1)S(1)}, u32[]{:S(2)}, u32[]{:S(2)}) collective-permute-start(bf16[256,256]{1,0:T(8,128)(2,1)S(1)} %slice.8), channel_id=1, source_target_pairs={{0,16},{8,24},{16,32},{24,40},{32,48},{40,56},{48,64},{56,72},{64,... | collective-permute-start | bytes 393224 | tf_op jit(solution)/shard_map/ppermute | solution.py:25
  23.9 3.7 %copy-start.2 = (bf16[128,1024]{1,0:T(8,128)(2,1)S(1)}, bf16[128,1024]{1,0:T(8,128)(2,1)}, u32[]{:S(2)}) copy-start(bf16[128,1024]{1,0:T(8,128)(2,1)} %q_ref.3) | copy-start | bytes 786436
  23.9 3.7 %copy-start.3 = (bf16[128,1024]{1,0:T(8,128)(2,1)S(1)}, bf16[128,1024]{1,0:T(8,128)(2,1)}, u32[]{:S(2)}) copy-start(bf16[128,1024]{1,0:T(8,128)(2,1)} %do_ref.3) | copy-start | bytes 786436
  34.5 31.5 %all-to-all-start.1 = ((f32[64,2,128]{2,1,0:T(2,128)}), f32[64,2,128]{2,1,0:T(2,128)S(1)}, u32[]{:S(2)}, u32[]{:S(2)}) async-start(f32[64,2,128]{2,1,0:T(2,128)} %bitcast.6), calls=%async_computation.1 | async-start | bytes 131072 | tf_op jit(solution)/shard_map/all_to_all | solution.py:311
  52.0 9.4 %collective-permute-start.2 = (bf16[384,256]{1,0:T(8,128)(2,1)S(1)}, bf16[384,256]{1,0:T(8,128)(2,1)S(1)}, u32[]{:S(2)}, u32[]{:S(2)}) collective-permute-start(bf16[384,256]{1,0:T(8,128)(2,1)S(1)} %get-tuple-element.30), channel_id=1, source_target_pairs={{8,0},{16,8},{24,16},{32,24},{40,32},{48,40},{56,48},{64,56},{72,6... | collective-permute-start | bytes 589832 | tf_op jit(solution)/shard_map/ppermute | solution.py:25
  53.2 8.1 %collective-permute-start.3 = (bf16[256,256]{1,0:T(8,128)(2,1)S(1)}, bf16[256,256]{1,0:T(8,128)(2,1)S(1)}, u32[]{:S(2)}, u32[]{:S(2)}) collective-permute-start(bf16[256,256]{1,0:T(8,128)(2,1)S(1)} %get-tuple-element.31), channel_id=1, source_target_pairs={{16,0},{24,8},{32,16},{40,24},{48,32},{56,40},{64,48},{72,56},{80,... | collective-permute-start | bytes 393224 | tf_op jit(solution)/shard_map/ppermute | solution.py:25

commit v3 on v2

--- a/solution.py
+++ b/solution.py
@@ -11,7 +11,6 @@
 PAIRS = 4
 NEG = -1e30
 PAIRS_OF_BLOCKS = 64
-CHUNK = 48
 VMEM = pl.BlockSpec(memory_space=pltpu.VMEM)
 SMEM = pl.BlockSpec(memory_space=pltpu.SMEM)
 ANY = pl.BlockSpec(memory_space=pl.ANY)
@@ -63,7 +62,7 @@
         bias[b * 128 : (b + 1) * 128, :] = jnp.concatenate([tile, tile], axis=1)
 
 
-def layer(layer_id, sinks_ref, q_ref, do_ref, odd, places, bias, kd, vd, kt, ws, dss, dq_ref, sink_acc, dq_hbm, sems):
+def layer(layer_id, sinks_ref, q_ref, do_ref, odd, places, bias, kd, vd, kt, ws, dss, dq_ref, sink_acc, sends=(), send_sinks=None):
     blocks = len(places) - 1
     rows = blocks * 128
 
@@ -86,7 +85,7 @@
         vd[0, span, :] = v0.astype(BF16)
         vd[1, span, :] = v1.astype(BF16)
     lane = lax.broadcasted_iota(jnp.int32, (1, 256), 1)
-    sums, sends = [], []
+    sums = []
     for g in range(2):
         q2s, do2s = [], []
         for j in range(PAIRS):
@@ -110,24 +109,23 @@
             at = layer_id * 16 + 2 * p
             sink_acc[at : at + 1, :] = grad[:, :128]
             sink_acc[at + 1 : at + 2, :] = grad[:, 128:]
+        if g == 1 and send_sinks is not None:
+            send_sinks()
         q_all = jnp.concatenate(q2s, axis=0)
         do_all = jnp.concatenate(do2s, axis=0)
-        dk = dot(dss[:rows, :], q_all, ((1,), (0,)))
-        dv = dot(ws[:rows, :], do_all, ((1,), (0,)))
-        sums.append((dk + pltpu.roll(dk, 64, 1), dv + pltpu.roll(dv, 64, 1)))
         dqt = dot(kt[g, :, :rows], dss[:rows, :], ((1,), (0,)))
         for j in range(PAIRS):
             p = g * PAIRS + j
             both = jnp.concatenate([dqt[:, j * 256 : j * 256 + 128], dqt[:, j * 256 + 128 : j * 256 + 256]], axis=0)
             dq_ref[:, p * 128 : (p + 1) * 128] = jnp.transpose(both).astype(BF16)
-        cols = slice(g * 512, (g + 1) * 512)
-        sends.append(pltpu.make_async_copy(dq_ref.at[:, cols], dq_hbm.at[:, cols], sems.at[1 + g]))
-        sends[-1].start()
+        if sends:
+            sends[g].start()
+        dk = dot(dss[:rows, :], q_all, ((1,), (0,)))
+        dv = dot(ws[:rows, :], do_all, ((1,), (0,)))
+        sums.append((dk + pltpu.roll(dk, 64, 1), dv + pltpu.roll(dv, 64, 1)))
     low = low_lanes(rows)
     dk = jnp.where(low, sums[0][0], sums[1][0]) * (HEAD_DIM**-0.5)
     dv = jnp.where(low, sums[0][1], sums[1][1])
-    for send in sends:
-        send.wait()
     return dk, dv
 
 
@@ -138,11 +136,12 @@
 
 
 def window_kernel(
-    me_ref, sinks_hbm, seg_ref, q_ref, do_ref, own, far2,
-    dq_hbm, mine, back, sinks_ref, band_bias, sink_acc,
-    bias, kd, vd, kt, ws, dss, dq_ref, sems,
+    sinks_hbm, seg_ref, q_ref, do_ref, own, far2,
+    dq_ref, mine, back, sinks_ref, band_bias, sink_acc,
+    bias, kd, vd, kt, ws, dss, sems,
 ):
-    me, odd = me_ref[0], me_ref[1] == 1
+    odd = lax.axis_index("yh") == 1
+    me = lax.axis_index("pair") * 2 + lax.axis_index("yh")
     fetch = pltpu.make_async_copy(sinks_hbm, sinks_ref, sems.at[0])
     fetch.start()
     sink_acc[...] = jnp.zeros_like(sink_acc)
@@ -151,7 +150,7 @@
     fetch.wait()
     blocks = [(far2, 256, 0), (own, 0, 0), (own, 128, 0)]
     dk, dv = layer(
-        0, sinks_ref, q_ref, do_ref, odd, blocks, bias, kd, vd, kt, ws, dss, dq_ref, sink_acc, dq_hbm, sems
+        0, sinks_ref, q_ref, do_ref, odd, blocks, bias, kd, vd, kt, ws, dss, dq_ref, sink_acc
     )
     for at, grad in ((0, dk), (128, dv)):
         parts = shifted(grad, 2, odd)
@@ -161,15 +160,29 @@
 
 
 def band_kernel(
-    me_ref, sinks_ref, bias, q_ref, do_ref, own, far2, far4, win_back, win_acc,
-    dq_hbm, mine, back2, back4, sink_ref,
-    kd, vd, kt, ws, dss, dq_ref, sink_acc, sems,
+    sinks_ref, bias, q_ref, do_ref, own, far2, far4, win_back, win_acc, win_dq,
+    win_dq_hbm, dq_hbm, mine, back2, back4, sink_hbm,
+    kd, vd, kt, ws, dss, dq_ref, sink_acc, sink_ref, sems,
 ):
-    odd = me_ref[1] == 1
+    odd = lax.axis_index("yh") == 1
+    win_send = pltpu.make_async_copy(win_dq, win_dq_hbm, sems.at[0])
+    win_send.start()
     sink_acc[...] = win_acc[...]
     blocks = [(far4, 0, 0), (far4, 128, 0), (far2, 0, 0), (far2, 128, 0), (own, 0, 256), (own, 128, 256)]
+    halves = (slice(0, 512), slice(512, 1024))
+    sends = [
+        pltpu.make_async_copy(dq_ref.at[:, cols], dq_hbm.at[:, cols], sems.at[1 + g]) for g, cols in enumerate(halves)
+    ]
+    sink_send = pltpu.make_async_copy(sink_ref, sink_hbm, sems.at[3])
+
+    def send_sinks():
+        total = jnp.sum(jnp.transpose(sink_acc[...]), axis=0, keepdims=True)
+        row = lax.broadcasted_iota(jnp.int32, sink_ref.shape, 0)
+        sink_ref[...] = jnp.where(row % 2 == 0, total, 0.0)
+        sink_send.start()
+
     dk, dv = layer(
-        1, sinks_ref, q_ref, do_ref, odd, blocks, bias, kd, vd, kt, ws, dss, dq_ref, sink_acc, dq_hbm, sems
+        1, sinks_ref, q_ref, do_ref, odd, blocks, bias, kd, vd, kt, ws, dss, dq_ref, sink_acc, sends, send_sinks
     )
     for at, grad in ((0, dk), (128, dv)):
         parts = shifted(grad, CYCLE + 1, odd)
@@ -179,9 +192,8 @@
             back2[rows, at : at + 128] = parts[2 + half].astype(BF16)
             mine[rows, at : at + 128] = parts[4 + half]
     back2[256:, :] = win_back[...]
-    total = jnp.sum(jnp.transpose(sink_acc[...]), axis=0, keepdims=True)
-    row = lax.broadcasted_iota(jnp.int32, sink_ref.shape, 0)
-    sink_ref[...] = jnp.where(row % 2 == 0, total, 0.0)
+    for send in [win_send, sink_send] + sends:
+        send.wait()
 
 
 def scratch(rows):
@@ -195,7 +207,7 @@
     ]
 
 
-def window_call(me, sinks, seg, q, do, own, far2):
+def window_call(sinks, seg, q, do, own, far2):
     shape = jax.ShapeDtypeStruct
     return pl.pallas_call(
         window_kernel,
@@ -203,28 +215,29 @@
             shape((128, 1024), BF16), shape((256, 256), F32), shape((128, 256), BF16),
             shape((2, 16), F32), shape(((CYCLE + 1) * 128, 256), F32), shape((128, 128), F32),
         ),
-        in_specs=[SMEM, HBM] + [VMEM] * 5,
-        out_specs=[HBM] + [VMEM] * 5,
-        scratch_shapes=[pltpu.VMEM((256, 256), F32)] + scratch(256) + [pltpu.SemaphoreType.DMA((3,))],
+        in_specs=[HBM] + [VMEM] * 5,
+        out_specs=[VMEM] * 6,
+        scratch_shapes=[pltpu.VMEM((256, 256), F32)] + scratch(256)[:-1] + [pltpu.SemaphoreType.DMA((1,))],
         compiler_params=pltpu.CompilerParams(vmem_limit_bytes=14 << 20),
         cost_estimate=pl.CostEstimate(flops=2_000_000_000, bytes_accessed=1_000_000, transcendentals=500_000),
-    )(me, sinks, seg, q, do, own, far2)
-
-
-def band_call(me, sinks, bias, q, do, own, far2, far4, win_back, win_acc):
+    )(sinks, seg, q, do, own, far2)
+
+
+def band_call(sinks, bias, q, do, own, far2, far4, win_back, win_acc, win_dq):
     shape = jax.ShapeDtypeStruct
     return pl.pallas_call(
         band_kernel,
         out_shape=(
-            shape((128, 1024), BF16), shape((256, 256), F32), shape((384, 256), BF16), shape((256, 256), BF16),
+            shape((128, 1024), BF16), shape((128, 1024), BF16),
+            shape((256, 256), F32), shape((384, 256), BF16), shape((256, 256), BF16),
             shape((PAIRS_OF_BLOCKS * 2, 128), F32),
         ),
-        in_specs=[SMEM] + [VMEM] * 9,
-        out_specs=[HBM] + [VMEM] * 4,
-        scratch_shapes=scratch((CYCLE + 1) * 128) + [pltpu.VMEM((128, 128), F32), pltpu.SemaphoreType.DMA((3,))],
+        in_specs=[VMEM] * 10,
+        out_specs=[HBM] * 2 + [VMEM] * 3 + [HBM],
+        scratch_shapes=scratch((CYCLE + 1) * 128) + [pltpu.VMEM((128, 128), F32)] * 2 + [pltpu.SemaphoreType.DMA((4,))],
         compiler_params=pltpu.CompilerParams(vmem_limit_bytes=24 << 20),
         cost_estimate=pl.CostEstimate(flops=5_000_000_000, bytes_accessed=2_000_000, transcendentals=1_500_000),
-    )(me, sinks, bias, q, do, own, far2, far4, win_back, win_acc)
+    )(sinks, bias, q, do, own, far2, far4, win_back, win_acc, win_dq)
 
 
 def pack_kernel(wk, wv, fk, fv, out, held, sems):
@@ -254,17 +267,17 @@
         rows = slice(half * 128, (half + 1) * 128)
         band = (band_mine[rows, :] + back2[rows, :].astype(F32) + back4[rows, :].astype(F32)).astype(BF16)
         for t in range(4):
-            at = (half * 4 + t) * CHUNK
+            at = (half * 4 + t) * 32
             out[at : at + 32, :256] = win[half][t * 32 : (t + 1) * 32].astype(BF16)
-            out[at : at + 32, 256:] = band[t * 32 : (t + 1) * 32]
-            out[at + 32 : at + 48, :128] = sinks
-            out[at + 32 : at + 48, 128:] = jnp.zeros((16, 384), BF16)
-
-
-def unpack_kernel(me_ref, grads, wk, wv, fk, fv, sinks):
+            out[at : at + 32, 256:512] = band[t * 32 : (t + 1) * 32]
+            out[at : at + 16, 512:] = sinks
+            out[at + 16 : at + 32, 512:] = jnp.zeros((16, 128), BF16)
+
+
+def unpack_kernel(grads, wk, wv, fk, fv, sinks):
     def chunk(yh, t):
-        at = (yh * 4 + t) * CHUNK
-        return grads[at : at + 32, :].astype(F32)
+        at = (yh * 4 + t) * 32
+        return grads[at : at + 32, :512].astype(F32)
 
     for t in range(4):
         total = (chunk(0, t) + chunk(1, t)).astype(BF16)
@@ -272,8 +285,8 @@
             ref[:, t * 128 : (t + 1) * 128] = total[:, a * 128 : (a + 1) * 128]
     parts = jnp.zeros((16, 128), F32)
     for yh in range(2):
-        at = pl.multiple_of((yh * 4 + me_ref[2]) * CHUNK + 32, 16)
-        parts = parts + grads[pl.ds(at, 16), :128].astype(F32)
+        at = pl.multiple_of((yh * 4 + lax.axis_index("head")) * 32, 32)
+        parts = parts + grads[pl.ds(at, 16), 512:].astype(F32)
     total = jnp.sum(parts, axis=0, keepdims=True)
     sinks[0:1, :] = total[:, 0:16]
     sinks[1:2, :] = total[:, 16:32]
@@ -299,22 +312,20 @@
     banded = own[:, 256:]
     far2 = passed_along(jnp.concatenate([banded, own[128:, :256]], axis=0), "pair", 1)
     far4 = passed_along(banded, "pair", 2)
-    pair, yh, head = (lax.axis_index(axis).astype(jnp.int32) for axis in ("pair", "yh", "head"))
-    me = jnp.stack([pair * 2 + yh, yh, head])
     win_dq, win_mine, win_back, sink_vals, bias, win_acc = window_call(
-        me, sinks, segments.reshape(128, 128), win_q, win_dout, own, far2
-    )
-    full_dq, band_mine, back2, back4, sink_rows = band_call(
-        me, sink_vals, bias, full_q, full_dout, own, far2, far4, win_back, win_acc
+        sinks, segments.reshape(128, 128), win_q, win_dout, own, far2
+    )
+    win_dq, full_dq, band_mine, back2, back4, sink_rows = band_call(
+        sink_vals, bias, full_q, full_dout, own, far2, far4, win_back, win_acc, win_dq
     )
     back2, back4 = passed_along(back2, "pair", -1), passed_along(back4, "pair", -2)
     sink_terms = lax.all_to_all(sink_rows, "pair", split_axis=0, concat_axis=0, tiled=True)
     summed = local_call(
-        sum_kernel, shape((8 * CHUNK, 512), BF16), (win_mine, band_mine, back2, back4, sink_terms), [VMEM] * 5
+        sum_kernel, shape((256, 640), BF16), (win_mine, band_mine, back2, back4, sink_terms), [VMEM] * 5
     )
     grads = lax.all_to_all(summed, ("yh", "head"), split_axis=0, concat_axis=0, tiled=True)
     win_dk, win_dv, full_dk, full_dv, sink_grads = local_call(
-        unpack_kernel, (shape((32, 512), BF16),) * 4 + (shape((2, 16), F32),), (me, grads), [SMEM, VMEM]
+        unpack_kernel, (shape((32, 512), BF16),) * 4 + (shape((2, 16), F32),), (grads,), [VMEM]
     )
     return win_dq, win_dk, win_dv, full_dq, full_dk, full_dv, sink_grads
 

time: 82.8 us -> 79.6 us (0.961)
  Pallas kernels: 13.4 us -> 10.8 us
  blocking collectives: 31.8 us -> 30.9 us
    pallas_call x1, Pallas kernels: 3.69 us -> 2.56 us  [window_call(): pl.pallas_call(window_kernel, out_shape=(shape((128, 1024), BF16), shape(...]
    pallas_call x1, Pallas kernels: 6.88 us -> 5.95 us  [band_call(): pl.pallas_call(band_kernel, out_shape=(shape((128, 1024), BF16), shape((1...]
    all_to_all x1, blocking collectives: 15.1 us -> 14.2 us  [body(): lax.all_to_all(summed, ('yh', 'head'), split_axis=0, concat_axis=0, tiled...]
  transfers between devices with their start and end apart: 5 -> 5, of which waited for: 3 -> 4; matrix products, arithmetic and copies ran while one was open for 0% -> 0% of each run, Pallas kernels for 4% -> 3%
where the time goes in v3:
time: 79.6 us; the launch traced here: 79.2 us
  blocking collectives  30.9 us (39%)
  starting transfers between devices  23.6 us (30%)
  waiting for transfers between devices  13.1 us (16%)
  Pallas kernels  10.8 us (14%)
    all_to_all x1, starting transfers between devices, body(): lax.all_to_all(sink_rows, 'pair', split_axis=0, concat_axis=0, tiled=True)  17.6 us
    all_to_all x1, blocking collectives, body(): lax.all_to_all(packed, ('yh', 'head'), split_axis=0, concat_axis=0, tiled...  16.7 us
    all_to_all x1, blocking collectives, body(): lax.all_to_all(summed, ('yh', 'head'), split_axis=0, concat_axis=0, tiled...  14.2 us
    ppermute x4, waiting for transfers between devices, passed_along(): return lax.ppermute(shard, axis, pairs)  8.44 us
    ppermute x4, starting transfers between devices, passed_along(): return lax.ppermute(shard, axis, pairs)  5.98 us
    pallas_call x1, Pallas kernels, band_call(): pl.pallas_call(band_kernel, out_shape=(shape((128, 1024), BF16), shape((1...  5.95 us
    all_to_all x1, waiting for transfers between devices, body(): lax.all_to_all(sink_rows, 'pair', split_axis=0, concat_axis=0, tiled=True)  4.64 us
    pallas_call x1, Pallas kernels, window_call(): pl.pallas_call(window_kernel, out_shape=(shape((128, 1024), BF16), shape(...  2.56 us
  transfers between devices with their start and end apart: 5, of which 4 were waited for; matrix products, arithmetic and copies ran while one was open for 0% of the time, Pallas kernels for 3%

profile of v3, /device:TPU:1, one launch (start us, length us, event | category | flops | bytes accessed | tf_op | source)
XLA Modules:
  0.0 79.2 jit_solution(8483289463527492257)
XLA Ops:
  0.6 1.6 %shard_map.153 = bf16[256,512]{1,0:T(8,128)(2,1)} custom-call(bf16[32,512]{1,0:T(8,128)(2,1)} %wk.1, bf16[32,512]{1,0:T(8,128)(2,1)} %wv.1, bf16[32,512]{1,0:T(8,128)(2,1)} %fk.1, bf16[32,512]{1,0:T(8,128)(2,1)} %fv.1), custom_call_target="tpu_custom_call" | custom-call | flops 100000 | bytes 500000 | tf_op jit(solution)/shard_map/pallas_call | solution.py:296
  2.2 16.7 %all_to_all.33 = bf16[8,32,512]{2,1,0:T(8,128)(2,1)S(1)} all-to-all(bf16[8,32,512]{2,1,0:T(8,128)(2,1)} %bitcast.15), channel_id=1, replica_groups=mesh['pair'=64,'yh'=2,'head'=4] {'yh','head'}, dimensions={0} | all-to-all | bytes 524288 | tf_op jit(solution)/shard_map/all_to_all | solution.py:311
  18.9 0.0 copy-start.1
  18.9 0.0 copy-start
  18.9 0.0 copy-start.4
  19.0 0.0 copy-start.5
  19.0 1.4 %collective-permute-start = (bf16[384,256]{1,0:T(8,128)(2,1)S(1)}, bf16[384,256]{1,0:T(8,128)(2,1)S(1)}, u32[]{:S(2)}, u32[]{:S(2)}) collective-permute-start(bf16[384,256]{1,0:T(8,128)(2,1)S(1)} %pad_maximum_fusion), channel_id=1, source_target_pairs={{0,8},{8,16},{16,24},{24,32},{32,40},{40,48},{48,56},{56,64},{64,7... | collective-permute-start | bytes 589832 | tf_op jit(solution)/shard_map/ppermute | solution.py:24
  20.4 2.0 %collective-permute-start.1 = (bf16[256,256]{1,0:T(8,128)(2,1)S(1)}, bf16[256,256]{1,0:T(8,128)(2,1)S(1)}, u32[]{:S(2)}, u32[]{:S(2)}) collective-permute-start(bf16[256,256]{1,0:T(8,128)(2,1)S(1)} %slice.8), channel_id=1, source_target_pairs={{0,16},{8,24},{16,32},{24,40},{32,48},{40,56},{48,64},{56,72},{64,... | collective-permute-start | bytes 393224 | tf_op jit(solution)/shard_map/ppermute | solution.py:24
  22.4 1.5 %collective-permute-done.far2 = bf16[384,256]{1,0:T(8,128)(2,1)S(1)} collective-permute-done((bf16[384,256]{1,0:T(8,128)(2,1)S(1)}, bf16[384,256]{1,0:T(8,128)(2,1)S(1)}, u32[]{:S(2)}, u32[]{:S(2)}) %collective-permute-start) | collective-permute-done | bytes 196640 | tf_op jit(solution)/shard_map/ppermute | solution.py:24
  23.9 0.0 copy-done.1
  23.9 0.0 copy-done
  23.9 0.0 copy-done.4
  23.9 0.0 copy-done.5
  23.9 0.0 copy-start.2
  23.9 0.0 copy-start.3
  23.9 2.6 %shard_map.154 = (bf16[128,1024]{1,0:T(8,128)(2,1)S(1)}, f32[256,256]{1,0:T(8,128)S(1)}, bf16[128,256]{1,0:T(8,128)(2,1)S(1)}, f32[2,16]{1,0:T(2,128)S(1)}, f32[...) custom-call(f32[2,16]{1,0:T(2,128)S(1)} %copy-done.5, s32[128,128]{1,0:T(8,128)S(1)} %bitcast.14, ...), custom_call_target="tpu_custom_call" | custom-call | flops 2000000000 | bytes 1000000 | tf_op jit(solution)/shard_map/pallas_call | solution.py:212
  26.5 0.2 collective-permute-done.1.far4
  26.7 0.0 copy-done.2
  26.7 0.0 copy-done.3
  26.7 6.0 %shard_map.155 = (bf16[128,1024]{1,0:T(8,128)(2,1)}, bf16[128,1024]{1,0:T(8,128)(2,1)}, f32[256,256]{1,0:T(8,128)S(1)}, bf16[384,256]{1,0:T(8,128)(2,1)S(1)}, bf...) custom-call(f32[2,16]{1,0:T(2,128)S(1)} %get-tuple-element.24.sinks_ref, f32[640,256]{1,0:T(8,128)S(1)} %get-tuple-element.25.bias, ...), custom_call_target="tpu_custom_call" | custom-call | flops 5000000000 | bytes 2000000 | tf_op jit(solution)/shard_map/pallas_call | solution.py:228
  32.6 17.6 %all-to-all-start.1 = ((f32[64,2,128]{2,1,0:T(2,128)}), f32[64,2,128]{2,1,0:T(2,128)S(1)}, u32[]{:S(2)}, u32[]{:S(2)}) async-start(f32[64,2,128]{2,1,0:T(2,128)} %bitcast.3), calls=%async_computation.1 | async-start | bytes 131072 | tf_op jit(solution)/shard_map/all_to_all | solution.py:322
  50.2 1.3 %collective-permute-start.2 = (bf16[384,256]{1,0:T(8,128)(2,1)S(1)}, bf16[384,256]{1,0:T(8,128)(2,1)S(1)}, u32[]{:S(2)}, u32[]{:S(2)}) collective-permute-start(bf16[384,256]{1,0:T(8,128)(2,1)S(1)} %get-tuple-element.32), channel_id=1, source_target_pairs={{8,0},{16,8},{24,16},{32,24},{40,32},{48,40},{56,48},{64,56},{72,6... | collective-permute-start | bytes 589832 | tf_op jit(solution)/shard_map/ppermute | solution.py:24
  51.5 1.3 %collective-permute-start.3 = (bf16[256,256]{1,0:T(8,128)(2,1)S(1)}, bf16[256,256]{1,0:T(8,128)(2,1)S(1)}, u32[]{:S(2)}, u32[]{:S(2)}) collective-permute-start(bf16[256,256]{1,0:T(8,128)(2,1)S(1)} %get-tuple-element.33), channel_id=1, source_target_pairs={{16,0},{24,8},{32,16},{40,24},{48,32},{56,40},{64,48},{72,56},{80,... | collective-permute-start | bytes 393224 | tf_op jit(solution)/shard_map/ppermute | solution.py:24
  52.8 6.8 %collective-permute-done.3.back4 = bf16[256,256]{1,0:T(8,128)(2,1)S(1)} collective-permute-done((bf16[256,256]{1,0:T(8,128)(2,1)S(1)}, bf16[256,256]{1,0:T(8,128)(2,1)S(1)}, u32[]{:S(2)}, u32[]{:S(2)}) %collective-permute-start.3) | collective-permute-done | bytes 131104 | tf_op jit(solution)/shard_map/ppermute | solution.py:24
  59.6 0.0 collective-permute-done.2.back2
  59.6 4.6 %all-to-all-done.1 = f32[64,2,128]{2,1,0:T(2,128)S(1)} async-done(((f32[64,2,128]{2,1,0:T(2,128)}), f32[64,2,128]{2,1,0:T(2,128)S(1)}, u32[]{:S(2)}, u32[]{:S(2)}) %all-to-all-start.1) | async-done | bytes 65568 | tf_op jit(solution)/shard_map/all_to_all | solution.py:322
  64.2 0.1 shard_map.156
  64.3 14.2 %all_to_all.34 = bf16[8,32,640]{2,1,0:T(8,128)(2,1)S(1)} all-to-all(bf16[8,32,640]{2,1,0:T(8,128)(2,1)S(1)} %bitcast.8), channel_id=1, replica_groups=mesh['pair'=64,'yh'=2,'head'=4] {'yh','head'}, dimensions={0} | all-to-all | bytes 655360 | tf_op jit(solution)/shard_map/all_to_all | solution.py:326
  78.5 0.7 shard_map.157
  (3 shorter events, 0.0 us)
Async XLA Ops:
  18.9 5.0 %copy-start.1 = (bf16[128,1024]{1,0:T(8,128)(2,1)S(1)}, bf16[128,1024]{1,0:T(8,128)(2,1)}, u32[]{:S(2)}) copy-start(bf16[128,1024]{1,0:T(8,128)(2,1)} %do_ref.2) | copy-start | bytes 786436
  18.9 4.9 %copy-start = (bf16[128,1024]{1,0:T(8,128)(2,1)S(1)}, bf16[128,1024]{1,0:T(8,128)(2,1)}, u32[]{:S(2)}) copy-start(bf16[128,1024]{1,0:T(8,128)(2,1)} %q_ref.2) | copy-start | bytes 786436
  18.9 4.9 %copy-start.4 = (s32[16384]{0:T(1024)S(1)}, s32[16384]{0:T(1024)}, u32[]{:S(2)}) copy-start(s32[16384]{0:T(1024)} %param.19) | copy-start | bytes 196612
  19.0 4.9 %copy-start.5 = (f32[2,16]{1,0:T(2,128)S(1)}, f32[2,16]{1,0:T(2,128)}, u32[]{:S(2)}) copy-start(f32[2,16]{1,0:T(2,128)} %sinks_hbm.1) | copy-start | bytes 388
  19.0 4.9 %collective-permute-start = (bf16[384,256]{1,0:T(8,128)(2,1)S(1)}, bf16[384,256]{1,0:T(8,128)(2,1)S(1)}, u32[]{:S(2)}, u32[]{:S(2)}) collective-permute-start(bf16[384,256]{1,0:T(8,128)(2,1)S(1)} %pad_maximum_fusion), channel_id=1, source_target_pairs={{0,8},{8,16},{16,24},{24,32},{32,40},{40,48},{48,56},{56,64},{64,7... | collective-permute-start | bytes 589832 | tf_op jit(solution)/shard_map/ppermute | solution.py:24
  20.4 6.2 %collective-permute-start.1 = (bf16[256,256]{1,0:T(8,128)(2,1)S(1)}, bf16[256,256]{1,0:T(8,128)(2,1)S(1)}, u32[]{:S(2)}, u32[]{:S(2)}) collective-permute-start(bf16[256,256]{1,0:T(8,128)(2,1)S(1)} %slice.8), channel_id=1, source_target_pairs={{0,16},{8,24},{16,32},{24,40},{32,48},{40,56},{48,64},{56,72},{64,... | collective-permute-start | bytes 393224 | tf_op jit(solution)/shard_map/ppermute | solution.py:24
  23.9 2.8 %copy-start.2 = (bf16[128,1024]{1,0:T(8,128)(2,1)S(1)}, bf16[128,1024]{1,0:T(8,128)(2,1)}, u32[]{:S(2)}) copy-start(bf16[128,1024]{1,0:T(8,128)(2,1)} %q_ref.3) | copy-start | bytes 786436
  23.9 2.8 %copy-start.3 = (bf16[128,1024]{1,0:T(8,128)(2,1)S(1)}, bf16[128,1024]{1,0:T(8,128)(2,1)}, u32[]{:S(2)}) copy-start(bf16[128,1024]{1,0:T(8,128)(2,1)} %do_ref.3) | copy-start | bytes 786436
  32.6 31.6 %all-to-all-start.1 = ((f32[64,2,128]{2,1,0:T(2,128)}), f32[64,2,128]{2,1,0:T(2,128)S(1)}, u32[]{:S(2)}, u32[]{:S(2)}) async-start(f32[64,2,128]{2,1,0:T(2,128)} %bitcast.3), calls=%async_computation.1 | async-start | bytes 131072 | tf_op jit(solution)/shard_map/all_to_all | solution.py:322
  50.2 9.4 %collective-permute-start.2 = (bf16[384,256]{1,0:T(8,128)(2,1)S(1)}, bf16[384,256]{1,0:T(8,128)(2,1)S(1)}, u32[]{:S(2)}, u32[]{:S(2)}) collective-permute-start(bf16[384,256]{1,0:T(8,128)(2,1)S(1)} %get-tuple-element.32), channel_id=1, source_target_pairs={{8,0},{16,8},{24,16},{32,24},{40,32},{48,40},{56,48},{64,56},{72,6... | collective-permute-start | bytes 589832 | tf_op jit(solution)/shard_map/ppermute | solution.py:24
  51.5 8.1 %collective-permute-start.3 = (bf16[256,256]{1,0:T(8,128)(2,1)S(1)}, bf16[256,256]{1,0:T(8,128)(2,1)S(1)}, u32[]{:S(2)}, u32[]{:S(2)}) collective-permute-start(bf16[256,256]{1,0:T(8,128)(2,1)S(1)} %get-tuple-element.33), channel_id=1, source_target_pairs={{16,0},{24,8},{32,16},{40,24},{48,32},{56,40},{64,48},{72,56},{80,... | collective-permute-start | bytes 393224 | tf_op jit(solution)/shard_map/ppermute | solution.py:24

commit v4 on v3

--- a/solution.py
+++ b/solution.py
@@ -307,7 +307,7 @@
 def body(win_q, win_k, win_v, win_dout, full_q, full_k, full_v, full_dout, sinks, segments):
     shape = jax.ShapeDtypeStruct
     held = [pltpu.VMEM((4, 32, 512), BF16), pltpu.SemaphoreType.DMA((4,))]
-    packed = local_call(pack_kernel, shape((256, 512), BF16), (win_k, win_v, full_k, full_v), [HBM] * 4, held, vmem=60)
+    packed = local_call(pack_kernel, shape((256, 512), BF16), [pltpu.with_memory_space_constraint(x, pltpu.HBM) for x in (win_k, win_v, full_k, full_v)], [HBM] * 4, held)
     own = lax.all_to_all(packed, ("yh", "head"), split_axis=0, concat_axis=0, tiled=True)
     banded = own[:, 256:]
     far2 = passed_along(jnp.concatenate([banded, own[128:, :256]], axis=0), "pair", 1)

time: 79.6 us -> 78.7 us (0.989)
  starting transfers between devices: 23.6 us -> 25 us
  blocking collectives: 30.9 us -> 30 us
    all_to_all x1, blocking collectives: 16.7 us -> 15.8 us  [body(): lax.all_to_all(packed, ('yh', 'head'), split_axis=0, concat_axis=0, tiled...]
where the time goes in v4:
time: 78.7 us; the launch traced here: 78.3 us
  blocking collectives  30 us (38%)
  starting transfers between devices  25 us (32%)
  waiting for transfers between devices  12.4 us (16%)
  Pallas kernels  10.1 us (13%)
    all_to_all x1, starting transfers between devices, body(): lax.all_to_all(sink_rows, 'pair', split_axis=0, concat_axis=0, tiled=True)  18.3 us
    all_to_all x1, blocking collectives, body(): lax.all_to_all(packed, ('yh', 'head'), split_axis=0, concat_axis=0, tiled...  15.8 us
    all_to_all x1, blocking collectives, body(): lax.all_to_all(summed, ('yh', 'head'), split_axis=0, concat_axis=0, tiled...  14.2 us
    ppermute x4, waiting for transfers between devices, passed_along(): return lax.ppermute(shard, axis, pairs)  7.73 us
    ppermute x4, starting transfers between devices, passed_along(): return lax.ppermute(shard, axis, pairs)  6.69 us
    pallas_call x1, Pallas kernels, band_call(): pl.pallas_call(band_kernel, out_shape=(shape((128, 1024), BF16), shape((1...  5.95 us
    all_to_all x1, waiting for transfers between devices, body(): lax.all_to_all(sink_rows, 'pair', split_axis=0, concat_axis=0, tiled=True)  4.64 us
    pallas_call x1, Pallas kernels, window_call(): pl.pallas_call(window_kernel, out_shape=(shape((128, 1024), BF16), shape(...  2.56 us
  transfers between devices with their start and end apart: 5, of which 4 were waited for; matrix products, arithmetic and copies ran while one was open for 0% of the time, Pallas kernels for 3%

profile of v4, /device:TPU:1, one launch (start us, length us, event | category | flops | bytes accessed | tf_op | source)
XLA Modules:
  0.0 78.3 jit_solution(5224133997126379892)
XLA Ops:
  0.6 0.9 %shard_map.153 = bf16[256,512]{1,0:T(8,128)(2,1)S(1)} custom-call(bf16[32,512]{1,0:T(8,128)(2,1)} %wk.1, bf16[32,512]{1,0:T(8,128)(2,1)} %wv.1, bf16[32,512]{1,0:T(8,128)(2,1)} %fk.1, bf16[32,512]{1,0:T(8,128)(2,1)} %fv.1), custom_call_target="tpu_custom_call" | custom-call | flops 100000 | bytes 500000 | tf_op jit(solution)/shard_map/pallas_call | solution.py:296
  1.5 15.8 %all_to_all.33 = bf16[8,32,512]{2,1,0:T(8,128)(2,1)S(1)} all-to-all(bf16[8,32,512]{2,1,0:T(8,128)(2,1)S(1)} %bitcast.9), channel_id=1, replica_groups=mesh['pair'=64,'yh'=2,'head'=4] {'yh','head'}, dimensions={0} | all-to-all | bytes 524288 | tf_op jit(solution)/shard_map/all_to_all | solution.py:311
  17.3 0.0 copy-start.1
  17.3 0.0 copy-start
  17.3 0.0 copy-start.4
  17.4 0.0 copy-start.5
  17.4 1.4 %collective-permute-start = (bf16[384,256]{1,0:T(8,128)(2,1)S(1)}, bf16[384,256]{1,0:T(8,128)(2,1)S(1)}, u32[]{:S(2)}, u32[]{:S(2)}) collective-permute-start(bf16[384,256]{1,0:T(8,128)(2,1)S(1)} %pad_maximum_fusion), channel_id=1, source_target_pairs={{0,8},{8,16},{16,24},{24,32},{32,40},{40,48},{48,56},{56,64},{64,7... | collective-permute-start | bytes 589832 | tf_op jit(solution)/shard_map/ppermute | solution.py:24
  18.8 2.7 %collective-permute-start.1 = (bf16[256,256]{1,0:T(8,128)(2,1)S(1)}, bf16[256,256]{1,0:T(8,128)(2,1)S(1)}, u32[]{:S(2)}, u32[]{:S(2)}) collective-permute-start(bf16[256,256]{1,0:T(8,128)(2,1)S(1)} %slice.8), channel_id=1, source_target_pairs={{0,16},{8,24},{16,32},{24,40},{32,48},{40,56},{48,64},{56,72},{64,... | collective-permute-start | bytes 393224 | tf_op jit(solution)/shard_map/ppermute | solution.py:24
  21.5 0.8 collective-permute-done.far2
  22.2 0.0 copy-done.1
  22.2 0.0 copy-done
  22.3 0.0 copy-done.4
  22.3 0.0 copy-done.5
  22.3 0.0 copy-start.2
  22.3 0.0 copy-start.3
  22.3 2.6 %shard_map.154 = (bf16[128,1024]{1,0:T(8,128)(2,1)S(1)}, f32[256,256]{1,0:T(8,128)S(1)}, bf16[128,256]{1,0:T(8,128)(2,1)S(1)}, f32[2,16]{1,0:T(2,128)S(1)}, f32[...) custom-call(f32[2,16]{1,0:T(2,128)S(1)} %copy-done.5, s32[128,128]{1,0:T(8,128)S(1)} %bitcast.15, ...), custom_call_target="tpu_custom_call" | custom-call | flops 2000000000 | bytes 1000000 | tf_op jit(solution)/shard_map/pallas_call | solution.py:212
  24.9 0.2 collective-permute-done.1.far4
  25.1 0.0 copy-done.2
  25.1 0.0 copy-done.3
  25.1 5.9 %shard_map.155 = (bf16[128,1024]{1,0:T(8,128)(2,1)}, bf16[128,1024]{1,0:T(8,128)(2,1)}, f32[256,256]{1,0:T(8,128)S(1)}, bf16[384,256]{1,0:T(8,128)(2,1)S(1)}, bf...) custom-call(f32[2,16]{1,0:T(2,128)S(1)} %get-tuple-element.24.sinks_ref, f32[640,256]{1,0:T(8,128)S(1)} %get-tuple-element.25.bias, ...), custom_call_target="tpu_custom_call" | custom-call | flops 5000000000 | bytes 2000000 | tf_op jit(solution)/shard_map/pallas_call | solution.py:228
  31.0 18.3 %all-to-all-start.1 = ((f32[64,2,128]{2,1,0:T(2,128)}), f32[64,2,128]{2,1,0:T(2,128)S(1)}, u32[]{:S(2)}, u32[]{:S(2)}) async-start(f32[64,2,128]{2,1,0:T(2,128)} %bitcast.3), calls=%async_computation.1 | async-start | bytes 131072 | tf_op jit(solution)/shard_map/all_to_all | solution.py:322
  49.3 1.3 %collective-permute-start.2 = (bf16[384,256]{1,0:T(8,128)(2,1)S(1)}, bf16[384,256]{1,0:T(8,128)(2,1)S(1)}, u32[]{:S(2)}, u32[]{:S(2)}) collective-permute-start(bf16[384,256]{1,0:T(8,128)(2,1)S(1)} %get-tuple-element.32), channel_id=1, source_target_pairs={{8,0},{16,8},{24,16},{32,24},{40,32},{48,40},{56,48},{64,56},{72,6... | collective-permute-start | bytes 589832 | tf_op jit(solution)/shard_map/ppermute | solution.py:24
  50.6 1.3 %collective-permute-start.3 = (bf16[256,256]{1,0:T(8,128)(2,1)S(1)}, bf16[256,256]{1,0:T(8,128)(2,1)S(1)}, u32[]{:S(2)}, u32[]{:S(2)}) collective-permute-start(bf16[256,256]{1,0:T(8,128)(2,1)S(1)} %get-tuple-element.33), channel_id=1, source_target_pairs={{16,0},{24,8},{32,16},{40,24},{48,32},{56,40},{64,48},{72,56},{80,... | collective-permute-start | bytes 393224 | tf_op jit(solution)/shard_map/ppermute | solution.py:24
  51.9 6.8 %collective-permute-done.3.back4 = bf16[256,256]{1,0:T(8,128)(2,1)S(1)} collective-permute-done((bf16[256,256]{1,0:T(8,128)(2,1)S(1)}, bf16[256,256]{1,0:T(8,128)(2,1)S(1)}, u32[]{:S(2)}, u32[]{:S(2)}) %collective-permute-start.3) | collective-permute-done | bytes 131104 | tf_op jit(solution)/shard_map/ppermute | solution.py:24
  58.7 0.0 collective-permute-done.2.back2
  58.7 4.6 %all-to-all-done.1 = f32[64,2,128]{2,1,0:T(2,128)S(1)} async-done(((f32[64,2,128]{2,1,0:T(2,128)}), f32[64,2,128]{2,1,0:T(2,128)S(1)}, u32[]{:S(2)}, u32[]{:S(2)}) %all-to-all-start.1) | async-done | bytes 65568 | tf_op jit(solution)/shard_map/all_to_all | solution.py:322
  63.3 0.1 shard_map.156
  63.4 14.2 %all_to_all.34 = bf16[8,32,640]{2,1,0:T(8,128)(2,1)S(1)} all-to-all(bf16[8,32,640]{2,1,0:T(8,128)(2,1)S(1)} %bitcast.8), channel_id=1, replica_groups=mesh['pair'=64,'yh'=2,'head'=4] {'yh','head'}, dimensions={0} | all-to-all | bytes 655360 | tf_op jit(solution)/shard_map/all_to_all | solution.py:326
  77.6 0.7 shard_map.157
  (3 shorter events, 0.0 us)
Async XLA Ops:
  17.3 5.0 %copy-start.1 = (bf16[128,1024]{1,0:T(8,128)(2,1)S(1)}, bf16[128,1024]{1,0:T(8,128)(2,1)}, u32[]{:S(2)}) copy-start(bf16[128,1024]{1,0:T(8,128)(2,1)} %do_ref.2) | copy-start | bytes 786436
  17.3 4.9 %copy-start = (bf16[128,1024]{1,0:T(8,128)(2,1)S(1)}, bf16[128,1024]{1,0:T(8,128)(2,1)}, u32[]{:S(2)}) copy-start(bf16[128,1024]{1,0:T(8,128)(2,1)} %q_ref.2) | copy-start | bytes 786436
  17.3 4.9 %copy-start.4 = (s32[16384]{0:T(1024)S(1)}, s32[16384]{0:T(1024)}, u32[]{:S(2)}) copy-start(s32[16384]{0:T(1024)} %param.19) | copy-start | bytes 196612
  17.4 4.9 %copy-start.5 = (f32[2,16]{1,0:T(2,128)S(1)}, f32[2,16]{1,0:T(2,128)}, u32[]{:S(2)}) copy-start(f32[2,16]{1,0:T(2,128)} %sinks_hbm.1) | copy-start | bytes 388
  17.4 4.9 %collective-permute-start = (bf16[384,256]{1,0:T(8,128)(2,1)S(1)}, bf16[384,256]{1,0:T(8,128)(2,1)S(1)}, u32[]{:S(2)}, u32[]{:S(2)}) collective-permute-start(bf16[384,256]{1,0:T(8,128)(2,1)S(1)} %pad_maximum_fusion), channel_id=1, source_target_pairs={{0,8},{8,16},{16,24},{24,32},{32,40},{40,48},{48,56},{56,64},{64,7... | collective-permute-start | bytes 589832 | tf_op jit(solution)/shard_map/ppermute | solution.py:24
  18.8 6.2 %collective-permute-start.1 = (bf16[256,256]{1,0:T(8,128)(2,1)S(1)}, bf16[256,256]{1,0:T(8,128)(2,1)S(1)}, u32[]{:S(2)}, u32[]{:S(2)}) collective-permute-start(bf16[256,256]{1,0:T(8,128)(2,1)S(1)} %slice.8), channel_id=1, source_target_pairs={{0,16},{8,24},{16,32},{24,40},{32,48},{40,56},{48,64},{56,72},{64,... | collective-permute-start | bytes 393224 | tf_op jit(solution)/shard_map/ppermute | solution.py:24
  22.3 2.8 %copy-start.2 = (bf16[128,1024]{1,0:T(8,128)(2,1)S(1)}, bf16[128,1024]{1,0:T(8,128)(2,1)}, u32[]{:S(2)}) copy-start(bf16[128,1024]{1,0:T(8,128)(2,1)} %q_ref.3) | copy-start | bytes 786436
  22.3 2.8 %copy-start.3 = (bf16[128,1024]{1,0:T(8,128)(2,1)S(1)}, bf16[128,1024]{1,0:T(8,128)(2,1)}, u32[]{:S(2)}) copy-start(bf16[128,1024]{1,0:T(8,128)(2,1)} %do_ref.3) | copy-start | bytes 786436
  31.0 32.3 %all-to-all-start.1 = ((f32[64,2,128]{2,1,0:T(2,128)}), f32[64,2,128]{2,1,0:T(2,128)S(1)}, u32[]{:S(2)}, u32[]{:S(2)}) async-start(f32[64,2,128]{2,1,0:T(2,128)} %bitcast.3), calls=%async_computation.1 | async-start | bytes 131072 | tf_op jit(solution)/shard_map/all_to_all | solution.py:322
  49.3 9.4 %collective-permute-start.2 = (bf16[384,256]{1,0:T(8,128)(2,1)S(1)}, bf16[384,256]{1,0:T(8,128)(2,1)S(1)}, u32[]{:S(2)}, u32[]{:S(2)}) collective-permute-start(bf16[384,256]{1,0:T(8,128)(2,1)S(1)} %get-tuple-element.32), channel_id=1, source_target_pairs={{8,0},{16,8},{24,16},{32,24},{40,32},{48,40},{56,48},{64,56},{72,6... | collective-permute-start | bytes 589832 | tf_op jit(solution)/shard_map/ppermute | solution.py:24
  50.6 8.1 %collective-permute-start.3 = (bf16[256,256]{1,0:T(8,128)(2,1)S(1)}, bf16[256,256]{1,0:T(8,128)(2,1)S(1)}, u32[]{:S(2)}, u32[]{:S(2)}) collective-permute-start(bf16[256,256]{1,0:T(8,128)(2,1)S(1)} %get-tuple-element.33), channel_id=1, source_target_pairs={{16,0},{24,8},{32,16},{40,24},{48,32},{56,40},{64,48},{72,56},{80,... | collective-permute-start | bytes 393224 | tf_op jit(solution)/shard_map/ppermute | solution.py:24

commit v5 on v4

--- a/solution.py
+++ b/solution.py
@@ -62,7 +62,7 @@
         bias[b * 128 : (b + 1) * 128, :] = jnp.concatenate([tile, tile], axis=1)
 
 
-def layer(layer_id, sinks_ref, q_ref, do_ref, odd, places, bias, kd, vd, kt, ws, dss, dq_ref, sink_acc, sends=(), send_sinks=None):
+def layer(layer_id, sinks_ref, q_ref, do_ref, odd, places, bias, kd, vd, kt, ws, dss, dq_ref, sink_acc, send_sinks=None):
     blocks = len(places) - 1
     rows = blocks * 128
 
@@ -118,8 +118,6 @@
             p = g * PAIRS + j
             both = jnp.concatenate([dqt[:, j * 256 : j * 256 + 128], dqt[:, j * 256 + 128 : j * 256 + 256]], axis=0)
             dq_ref[:, p * 128 : (p + 1) * 128] = jnp.transpose(both).astype(BF16)
-        if sends:
-            sends[g].start()
         dk = dot(dss[:rows, :], q_all, ((1,), (0,)))
         dv = dot(ws[:rows, :], do_all, ((1,), (0,)))
         sums.append((dk + pltpu.roll(dk, 64, 1), dv + pltpu.roll(dv, 64, 1)))
@@ -161,19 +159,15 @@
 
 def band_kernel(
     sinks_ref, bias, q_ref, do_ref, own, far2, far4, win_back, win_acc, win_dq,
-    win_dq_hbm, dq_hbm, mine, back2, back4, sink_hbm,
-    kd, vd, kt, ws, dss, dq_ref, sink_acc, sink_ref, sems,
+    win_dq_hbm, dq_ref, mine, back2, back4, sink_hbm,
+    kd, vd, kt, ws, dss, sink_acc, sink_ref, sems,
 ):
     odd = lax.axis_index("yh") == 1
     win_send = pltpu.make_async_copy(win_dq, win_dq_hbm, sems.at[0])
     win_send.start()
     sink_acc[...] = win_acc[...]
     blocks = [(far4, 0, 0), (far4, 128, 0), (far2, 0, 0), (far2, 128, 0), (own, 0, 256), (own, 128, 256)]
-    halves = (slice(0, 512), slice(512, 1024))
-    sends = [
-        pltpu.make_async_copy(dq_ref.at[:, cols], dq_hbm.at[:, cols], sems.at[1 + g]) for g, cols in enumerate(halves)
-    ]
-    sink_send = pltpu.make_async_copy(sink_ref, sink_hbm, sems.at[3])
+    sink_send = pltpu.make_async_copy(sink_ref, sink_hbm, sems.at[1])
 
     def send_sinks():
         total = jnp.sum(jnp.transpose(sink_acc[...]), axis=0, keepdims=True)
@@ -182,7 +176,7 @@
         sink_send.start()
 
     dk, dv = layer(
-        1, sinks_ref, q_ref, do_ref, odd, blocks, bias, kd, vd, kt, ws, dss, dq_ref, sink_acc, sends, send_sinks
+        1, sinks_ref, q_ref, do_ref, odd, blocks, bias, kd, vd, kt, ws, dss, dq_ref, sink_acc, send_sinks
     )
     for at, grad in ((0, dk), (128, dv)):
         parts = shifted(grad, CYCLE + 1, odd)
@@ -192,8 +186,8 @@
             back2[rows, at : at + 128] = parts[2 + half].astype(BF16)
             mine[rows, at : at + 128] = parts[4 + half]
     back2[256:, :] = win_back[...]
-    for send in [win_send, sink_send] + sends:
-        send.wait()
+    win_send.wait()
+    sink_send.wait()
 
 
 def scratch(rows):
@@ -233,8 +227,8 @@
             shape((PAIRS_OF_BLOCKS * 2, 128), F32),
         ),
         in_specs=[VMEM] * 10,
-        out_specs=[HBM] * 2 + [VMEM] * 3 + [HBM],
-        scratch_shapes=scratch((CYCLE + 1) * 128) + [pltpu.VMEM((128, 128), F32)] * 2 + [pltpu.SemaphoreType.DMA((4,))],
+        out_specs=[HBM] + [VMEM] * 4 + [HBM],
+        scratch_shapes=scratch((CYCLE + 1) * 128)[:-1] + [pltpu.VMEM((128, 128), F32)] * 2 + [pltpu.SemaphoreType.DMA((2,))],
         compiler_params=pltpu.CompilerParams(vmem_limit_bytes=24 << 20),
         cost_estimate=pl.CostEstimate(flops=5_000_000_000, bytes_accessed=2_000_000, transcendentals=1_500_000),
     )(sinks, bias, q, do, own, far2, far4, win_back, win_acc, win_dq)
@@ -274,7 +268,10 @@
             out[at + 16 : at + 32, 512:] = jnp.zeros((16, 128), BF16)
 
 
-def unpack_kernel(grads, wk, wv, fk, fv, sinks):
+def unpack_kernel(grads, dq_ref, wk, wv, fk, fv, sinks, dq_hbm, sem):
+    send = pltpu.make_async_copy(dq_ref, dq_hbm, sem)
+    send.start()
+
     def chunk(yh, t):
         at = (yh * 4 + t) * 32
         return grads[at : at + 32, :512].astype(F32)
@@ -290,6 +287,7 @@
     total = jnp.sum(parts, axis=0, keepdims=True)
     sinks[0:1, :] = total[:, 0:16]
     sinks[1:2, :] = total[:, 16:32]
+    send.wait()
 
 
 def local_call(kernel, out_shape, args, in_specs, scratch_shapes=(), flops=100_000, vmem=4):
@@ -315,7 +313,7 @@
     win_dq, win_mine, win_back, sink_vals, bias, win_acc = window_call(
         sinks, segments.reshape(128, 128), win_q, win_dout, own, far2
     )
-    win_dq, full_dq, band_mine, back2, back4, sink_rows = band_call(
+    win_dq, band_dq, band_mine, back2, back4, sink_rows = band_call(
         sink_vals, bias, full_q, full_dout, own, far2, far4, win_back, win_acc, win_dq
     )
     back2, back4 = passed_along(back2, "pair", -1), passed_along(back4, "pair", -2)
@@ -324,9 +322,16 @@
         sum_kernel, shape((256, 640), BF16), (win_mine, band_mine, back2, back4, sink_terms), [VMEM] * 5
     )
     grads = lax.all_to_all(summed, ("yh", "head"), split_axis=0, concat_axis=0, tiled=True)
-    win_dk, win_dv, full_dk, full_dv, sink_grads = local_call(
-        unpack_kernel, (shape((32, 512), BF16),) * 4 + (shape((2, 16), F32),), (grads,), [VMEM]
-    )
+    part = shape((32, 512), BF16)
+    win_dk, win_dv, full_dk, full_dv, sink_grads, full_dq = pl.pallas_call(
+        unpack_kernel,
+        out_shape=(part,) * 4 + (shape((2, 16), F32), shape((128, 1024), BF16)),
+        in_specs=[VMEM] * 2,
+        out_specs=[VMEM] * 5 + [HBM],
+        scratch_shapes=[pltpu.SemaphoreType.DMA],
+        compiler_params=pltpu.CompilerParams(vmem_limit_bytes=4 << 20),
+        cost_estimate=pl.CostEstimate(flops=100_000, bytes_accessed=500_000, transcendentals=0),
+    )(grads, band_dq)
     return win_dq, win_dk, win_dv, full_dq, full_dk, full_dv, sink_grads
 
 

time: 78.7 us -> 79.3 us (level)
    pallas_call x0 -> x1, Pallas kernels: none -> 1.38 us  [body(): pl.pallas_call(unpack_kernel, out_shape=(part,) * 4 + (shape((2, 16), F32...]
where the time goes in v5:
time: 79.3 us; the launch traced here: 78.9 us
  blocking collectives  30 us (38%)
  starting transfers between devices  25 us (32%)
  waiting for transfers between devices  12.4 us (16%)
  Pallas kernels  10.7 us (13%)
    all_to_all x1, starting transfers between devices, body(): lax.all_to_all(sink_rows, 'pair', split_axis=0, concat_axis=0, tiled=True)  18.3 us
    all_to_all x1, blocking collectives, body(): lax.all_to_all(packed, ('yh', 'head'), split_axis=0, concat_axis=0, tiled...  15.8 us
    all_to_all x1, blocking collectives, body(): lax.all_to_all(summed, ('yh', 'head'), split_axis=0, concat_axis=0, tiled...  14.2 us
    ppermute x4, waiting for transfers between devices, passed_along(): return lax.ppermute(shard, axis, pairs)  7.73 us
    ppermute x4, starting transfers between devices, passed_along(): return lax.ppermute(shard, axis, pairs)  6.69 us
    pallas_call x1, Pallas kernels, band_call(): pl.pallas_call(band_kernel, out_shape=(shape((128, 1024), BF16), shape((1...  5.87 us
    all_to_all x1, waiting for transfers between devices, body(): lax.all_to_all(sink_rows, 'pair', split_axis=0, concat_axis=0, tiled=True)  4.64 us
    pallas_call x1, Pallas kernels, window_call(): pl.pallas_call(window_kernel, out_shape=(shape((128, 1024), BF16), shape(...  2.56 us
  transfers between devices with their start and end apart: 5, of which 4 were waited for; matrix products, arithmetic and copies ran while one was open for 0% of the time, Pallas kernels for 3%

profile of v5, /device:TPU:1, one launch (start us, length us, event | category | flops | bytes accessed | tf_op | source)
XLA Modules:
  0.0 78.9 jit_solution(5144348540370353809)
XLA Ops:
  0.6 0.9 %shard_map.153 = bf16[256,512]{1,0:T(8,128)(2,1)S(1)} custom-call(bf16[32,512]{1,0:T(8,128)(2,1)} %wk.1, bf16[32,512]{1,0:T(8,128)(2,1)} %wv.1, bf16[32,512]{1,0:T(8,128)(2,1)} %fk.1, bf16[32,512]{1,0:T(8,128)(2,1)} %fv.1), custom_call_target="tpu_custom_call" | custom-call | flops 100000 | bytes 500000 | tf_op jit(solution)/shard_map/pallas_call | solution.py:294
  1.5 15.8 %all_to_all.33 = bf16[8,32,512]{2,1,0:T(8,128)(2,1)S(1)} all-to-all(bf16[8,32,512]{2,1,0:T(8,128)(2,1)S(1)} %bitcast.9), channel_id=1, replica_groups=mesh['pair'=64,'yh'=2,'head'=4] {'yh','head'}, dimensions={0} | all-to-all | bytes 524288 | tf_op jit(solution)/shard_map/all_to_all | solution.py:309
  17.3 0.0 copy-start.1
  17.3 0.0 copy-start
  17.3 0.0 copy-start.4
  17.4 0.0 copy-start.5
  17.4 1.4 %collective-permute-start = (bf16[384,256]{1,0:T(8,128)(2,1)S(1)}, bf16[384,256]{1,0:T(8,128)(2,1)S(1)}, u32[]{:S(2)}, u32[]{:S(2)}) collective-permute-start(bf16[384,256]{1,0:T(8,128)(2,1)S(1)} %pad_maximum_fusion), channel_id=1, source_target_pairs={{0,8},{8,16},{16,24},{24,32},{32,40},{40,48},{48,56},{56,64},{64,7... | collective-permute-start | bytes 589832 | tf_op jit(solution)/shard_map/ppermute | solution.py:24
  18.8 2.7 %collective-permute-start.1 = (bf16[256,256]{1,0:T(8,128)(2,1)S(1)}, bf16[256,256]{1,0:T(8,128)(2,1)S(1)}, u32[]{:S(2)}, u32[]{:S(2)}) collective-permute-start(bf16[256,256]{1,0:T(8,128)(2,1)S(1)} %slice.8), channel_id=1, source_target_pairs={{0,16},{8,24},{16,32},{24,40},{32,48},{40,56},{48,64},{56,72},{64,... | collective-permute-start | bytes 393224 | tf_op jit(solution)/shard_map/ppermute | solution.py:24
  21.5 0.8 collective-permute-done.far2
  22.2 0.0 copy-done.1
  22.2 0.0 copy-done
  22.3 0.0 copy-done.4
  22.3 0.0 copy-done.5
  22.3 0.0 copy-start.2
  22.3 0.0 copy-start.3
  22.3 2.6 %shard_map.154 = (bf16[128,1024]{1,0:T(8,128)(2,1)S(1)}, f32[256,256]{1,0:T(8,128)S(1)}, bf16[128,256]{1,0:T(8,128)(2,1)S(1)}, f32[2,16]{1,0:T(2,128)S(1)}, f32[...) custom-call(f32[2,16]{1,0:T(2,128)S(1)} %copy-done.5, s32[128,128]{1,0:T(8,128)S(1)} %bitcast.15, ...), custom_call_target="tpu_custom_call" | custom-call | flops 2000000000 | bytes 1000000 | tf_op jit(solution)/shard_map/pallas_call | solution.py:206
  24.9 0.2 collective-permute-done.1.far4
  25.1 0.0 copy-done.2
  25.1 0.0 copy-done.3
  25.1 5.9 %shard_map.155 = (bf16[128,1024]{1,0:T(8,128)(2,1)}, bf16[128,1024]{1,0:T(8,128)(2,1)S(1)}, f32[256,256]{1,0:T(8,128)S(1)}, bf16[384,256]{1,0:T(8,128)(2,1)S(1)}...) custom-call(f32[2,16]{1,0:T(2,128)S(1)} %get-tuple-element.25.sinks_ref, f32[640,256]{1,0:T(8,128)S(1)} %get-tuple-element.26.bias, ...), custom_call_target="tpu_custom_call" | custom-call | flops 5000000000 | bytes 2000000 | tf_op jit(solution)/shard_map/pallas_call | solution.py:222
  30.9 18.3 %all-to-all-start.1 = ((f32[64,2,128]{2,1,0:T(2,128)}), f32[64,2,128]{2,1,0:T(2,128)S(1)}, u32[]{:S(2)}, u32[]{:S(2)}) async-start(f32[64,2,128]{2,1,0:T(2,128)} %bitcast.3), calls=%async_computation.1 | async-start | bytes 131072 | tf_op jit(solution)/shard_map/all_to_all | solution.py:320
  49.2 1.3 %collective-permute-start.2 = (bf16[384,256]{1,0:T(8,128)(2,1)S(1)}, bf16[384,256]{1,0:T(8,128)(2,1)S(1)}, u32[]{:S(2)}, u32[]{:S(2)}) collective-permute-start(bf16[384,256]{1,0:T(8,128)(2,1)S(1)} %get-tuple-element.33), channel_id=1, source_target_pairs={{8,0},{16,8},{24,16},{32,24},{40,32},{48,40},{56,48},{64,56},{72,6... | collective-permute-start | bytes 589832 | tf_op jit(solution)/shard_map/ppermute | solution.py:24
  50.5 1.3 %collective-permute-start.3 = (bf16[256,256]{1,0:T(8,128)(2,1)S(1)}, bf16[256,256]{1,0:T(8,128)(2,1)S(1)}, u32[]{:S(2)}, u32[]{:S(2)}) collective-permute-start(bf16[256,256]{1,0:T(8,128)(2,1)S(1)} %get-tuple-element.34), channel_id=1, source_target_pairs={{16,0},{24,8},{32,16},{40,24},{48,32},{56,40},{64,48},{72,56},{80,... | collective-permute-start | bytes 393224 | tf_op jit(solution)/shard_map/ppermute | solution.py:24
  51.8 6.8 %collective-permute-done.3.back4 = bf16[256,256]{1,0:T(8,128)(2,1)S(1)} collective-permute-done((bf16[256,256]{1,0:T(8,128)(2,1)S(1)}, bf16[256,256]{1,0:T(8,128)(2,1)S(1)}, u32[]{:S(2)}, u32[]{:S(2)}) %collective-permute-start.3) | collective-permute-done | bytes 131104 | tf_op jit(solution)/shard_map/ppermute | solution.py:24
  58.6 0.0 collective-permute-done.2.back2
  58.6 4.6 %all-to-all-done.1 = f32[64,2,128]{2,1,0:T(2,128)S(1)} async-done(((f32[64,2,128]{2,1,0:T(2,128)}), f32[64,2,128]{2,1,0:T(2,128)S(1)}, u32[]{:S(2)}, u32[]{:S(2)}) %all-to-all-start.1) | async-done | bytes 65568 | tf_op jit(solution)/shard_map/all_to_all | solution.py:320
  63.3 0.1 shard_map.156
  63.3 14.2 %all_to_all.34 = bf16[8,32,640]{2,1,0:T(8,128)(2,1)S(1)} all-to-all(bf16[8,32,640]{2,1,0:T(8,128)(2,1)S(1)} %bitcast.8), channel_id=1, replica_groups=mesh['pair'=64,'yh'=2,'head'=4] {'yh','head'}, dimensions={0} | all-to-all | bytes 655360 | tf_op jit(solution)/shard_map/all_to_all | solution.py:324
  77.5 1.4 %shard_map.157 = (bf16[32,512]{1,0:T(8,128)(2,1)}, bf16[32,512]{1,0:T(8,128)(2,1)}, bf16[32,512]{1,0:T(8,128)(2,1)}, bf16[32,512]{1,0:T(8,128)(2,1)}, f32[2,16]{1,0:T(2,128)}, /*index=5*/bf16[128,1024]{1,0:T(8,128)(2,1)}) custom-call(bf16[256,640]{1,0:T(8,128)(2,1)S(1)} %bitcast.7, bf16[128,1024]{1,0:T(8,128)(2,1)S(1)} %get-tuple-element.36.dq_ref), custom_call_target="tpu_custom_call" | custom-call | flops 100000 | bytes 500000 | tf_op jit(solution)/shard_map/pallas_call | solution.py:326
  (3 shorter events, 0.0 us)
Async XLA Ops:
  17.3 5.0 %copy-start.1 = (bf16[128,1024]{1,0:T(8,128)(2,1)S(1)}, bf16[128,1024]{1,0:T(8,128)(2,1)}, u32[]{:S(2)}) copy-start(bf16[128,1024]{1,0:T(8,128)(2,1)} %do_ref.2) | copy-start | bytes 786436
  17.3 4.9 %copy-start = (bf16[128,1024]{1,0:T(8,128)(2,1)S(1)}, bf16[128,1024]{1,0:T(8,128)(2,1)}, u32[]{:S(2)}) copy-start(bf16[128,1024]{1,0:T(8,128)(2,1)} %q_ref.2) | copy-start | bytes 786436
  17.3 4.9 %copy-start.4 = (s32[16384]{0:T(1024)S(1)}, s32[16384]{0:T(1024)}, u32[]{:S(2)}) copy-start(s32[16384]{0:T(1024)} %param.19) | copy-start | bytes 196612
  17.4 4.9 %copy-start.5 = (f32[2,16]{1,0:T(2,128)S(1)}, f32[2,16]{1,0:T(2,128)}, u32[]{:S(2)}) copy-start(f32[2,16]{1,0:T(2,128)} %sinks_hbm.1) | copy-start | bytes 388
  17.4 4.9 %collective-permute-start = (bf16[384,256]{1,0:T(8,128)(2,1)S(1)}, bf16[384,256]{1,0:T(8,128)(2,1)S(1)}, u32[]{:S(2)}, u32[]{:S(2)}) collective-permute-start(bf16[384,256]{1,0:T(8,128)(2,1)S(1)} %pad_maximum_fusion), channel_id=1, source_target_pairs={{0,8},{8,16},{16,24},{24,32},{32,40},{40,48},{48,56},{56,64},{64,7... | collective-permute-start | bytes 589832 | tf_op jit(solution)/shard_map/ppermute | solution.py:24
  18.8 6.2 %collective-permute-start.1 = (bf16[256,256]{1,0:T(8,128)(2,1)S(1)}, bf16[256,256]{1,0:T(8,128)(2,1)S(1)}, u32[]{:S(2)}, u32[]{:S(2)}) collective-permute-start(bf16[256,256]{1,0:T(8,128)(2,1)S(1)} %slice.8), channel_id=1, source_target_pairs={{0,16},{8,24},{16,32},{24,40},{32,48},{40,56},{48,64},{56,72},{64,... | collective-permute-start | bytes 393224 | tf_op jit(solution)/shard_map/ppermute | solution.py:24
  22.3 2.8 %copy-start.2 = (bf16[128,1024]{1,0:T(8,128)(2,1)S(1)}, bf16[128,1024]{1,0:T(8,128)(2,1)}, u32[]{:S(2)}) copy-start(bf16[128,1024]{1,0:T(8,128)(2,1)} %q_ref.3) | copy-start | bytes 786436
  22.3 2.8 %copy-start.3 = (bf16[128,1024]{1,0:T(8,128)(2,1)S(1)}, bf16[128,1024]{1,0:T(8,128)(2,1)}, u32[]{:S(2)}) copy-start(bf16[128,1024]{1,0:T(8,128)(2,1)} %do_ref.3) | copy-start | bytes 786436
  30.9 32.3 %all-to-all-start.1 = ((f32[64,2,128]{2,1,0:T(2,128)}), f32[64,2,128]{2,1,0:T(2,128)S(1)}, u32[]{:S(2)}, u32[]{:S(2)}) async-start(f32[64,2,128]{2,1,0:T(2,128)} %bitcast.3), calls=%async_computation.1 | async-start | bytes 131072 | tf_op jit(solution)/shard_map/all_to_all | solution.py:320
  49.2 9.4 %collective-permute-start.2 = (bf16[384,256]{1,0:T(8,128)(2,1)S(1)}, bf16[384,256]{1,0:T(8,128)(2,1)S(1)}, u32[]{:S(2)}, u32[]{:S(2)}) collective-permute-start(bf16[384,256]{1,0:T(8,128)(2,1)S(1)} %get-tuple-element.33), channel_id=1, source_target_pairs={{8,0},{16,8},{24,16},{32,24},{40,32},{48,40},{56,48},{64,56},{72,6... | collective-permute-start | bytes 589832 | tf_op jit(solution)/shard_map/ppermute | solution.py:24
  50.5 8.1 %collective-permute-start.3 = (bf16[256,256]{1,0:T(8,128)(2,1)S(1)}, bf16[256,256]{1,0:T(8,128)(2,1)S(1)}, u32[]{:S(2)}, u32[]{:S(2)}) collective-permute-start(bf16[256,256]{1,0:T(8,128)(2,1)S(1)} %get-tuple-element.34), channel_id=1, source_target_pairs={{16,0},{24,8},{32,16},{40,24},{48,32},{56,40},{64,48},{72,56},{80,... | collective-permute-start | bytes 393224 | tf_op jit(solution)/shard_map/ppermute | solution.py:24
